TPU v7x, 256 devices: a whole 4x4x8 slice. The times are simulated.
256 devices in a mesh: gx: 16 (over x_lo, z), gy: 8 (over y, core), gz: 2 (over x_hi).
Axes of the slice: x: 4 (x_hi: 2, x_lo: 2; x = x_hi * 2 + x_lo), y: 4, z: 8, core: 2. Of those that a mesh axis runs over, the one named last changes fastest.
Arguments:
- section_fields: float32 [25, 16, 512, 1024], P(None, 'gz', 'gx', 'gy'), may hold values from -4 to 4
- base_fields: float32 [25, 16, 512, 1024], P(None, 'gz', 'gx', 'gy'), may hold values from -6 to 6
- flags: int32 [16, 8], P('gx', 'gy'), may hold values 0 or 1
Outputs:
- next_fields: float32 [25, 16, 512, 1024], P(None, 'gz', 'gx', 'gy')
All inputs are finite; a program needn't handle non-finite values. No bound on the sum of `flags` on one device may be relied on, other than what follows from the above.
Results may differ from a plain program's by a relative error of at most 0.0001.
Values sent between devices are 32-bit elements; how exact they have to be, the bound alone decides.
A program may use at most 128 MiB of HBM per device.

v0:
```python
import jax
import jax.numpy as jnp
from jax import lax
from jax.sharding import PartitionSpec as P

PAIRS = ((0, 0), (0, 1), (0, 2), (1, 1), (1, 2), (2, 2))
SIGN_TABLE = (
    1.0,
    1.0,
    1.0,
    -1.0,
    1.0,
    -1.0,
    1.0,
    1.0,
    1.0,
    1.0,
    -1.0,
    1.0,
    -1.0,
    1.0,
    -1.0,
    -1.0,
    1.0,
    1.0,
    1.0,
    -1.0,
    -1.0,
    1.0,
    -1.0,
    -1.0,
    1.0,
)


def with_halo(array, sides, width, wrap):
    for axis, dim in sides:
        count, length = (lax.axis_size(axis), array.shape[dim])
        up = [(i, (i + 1) % count) for i in range(count if wrap else count - 1)]
        down = [(j, i) for i, j in up]
        last = lax.slice_in_dim(array, length - width, length, axis=dim)
        leading = lax.slice_in_dim(array, 0, width, axis=dim)
        before = lax.ppermute(last, axis, up)
        after = lax.ppermute(leading, axis, down)
        array = jnp.concatenate([before, array, after], axis=dim)
    return array


def from_partner(block, axis, stride):
    count = lax.axis_size(axis)
    route = []
    for low in range(count):
        high = low | 1 << stride
        if high != low and high < count:
            route += [(low, high), (high, low)]
    return lax.ppermute(block, axis, route)


def sym_index(i, j):
    return PAIRS.index((min(i, j), max(i, j)))


def differences(padded, axis, count):

    def shifted(k):
        return lax.slice_in_dim(padded, 3 + k, 3 + k + count, axis=axis)

    centre = shifted(0)
    first = (shifted(-2) - 8.0 * shifted(-1) + 8.0 * shifted(1) - shifted(2)) / 12.0
    second = (
        -shifted(-2) + 16.0 * shifted(-1) - 30.0 * centre + 16.0 * shifted(1) - shifted(2)
    ) / 12.0
    smooth = (
        shifted(-3)
        + shifted(3)
        - 6.0 * (shifted(-2) + shifted(2))
        + 15.0 * (shifted(-1) + shifted(1))
        - 20.0 * centre
    ) / 64.0
    return (first, second, smooth)


def evolve(state, first, second, smooth, sigma):
    conformal = state[0]
    trace_k = state[7]
    lapse = state[17]
    theta = state[18]

    def metric(i, j):
        return state[1 + sym_index(i, j)]

    def curv(i, j):
        return state[8 + sym_index(i, j)]

    def grad_shift(k, j):
        return first[j][19 + k]

    div = grad_shift(0, 0) + grad_shift(1, 1) + grad_shift(2, 2)
    lap = second[0][17] + second[1][17] + second[2][17]
    square = sum((curv(i, j) * curv(i, j) for i in range(3) for j in range(3)))
    rhs_chi = 2.0 / 3.0 * conformal * (lapse * trace_k - div)
    rhs_metric = []
    rhs_curv = []
    for i, j in PAIRS:
        lie_g = sum(
            (metric(i, k) * grad_shift(k, j) + metric(j, k) * grad_shift(k, i) for k in range(3))
        )
        rhs_metric.append(-2.0 * lapse * curv(i, j) + lie_g - 2.0 / 3.0 * metric(i, j) * div)
        lie_a = sum(
            (curv(i, k) * grad_shift(k, j) + curv(j, k) * grad_shift(k, i) for k in range(3))
        )
        quad = sum((curv(i, k) * curv(k, j) for k in range(3)))
        term = lapse * (trace_k * curv(i, j) - 2.0 * quad) + lie_a - 2.0 / 3.0 * curv(i, j) * div
        if i == j:
            term = term + conformal * (lap / 3.0 - second[i][17])
        rhs_curv.append(term)
    rhs_k = -conformal * lap + lapse * (square + trace_k * trace_k / 3.0)
    rhs_gamma = []
    for i in range(3):
        value = second[0][19 + i] + second[1][19 + i] + second[2][19 + i]
        value = value - 2.0 * sum((curv(i, j) * first[j][17] for j in range(3)))
        value = value + 2.0 / 3.0 * state[14 + i] * div
        value = value - sum((state[14 + j] * grad_shift(i, j) for j in range(3)))
        rhs_gamma.append(value)
    rhs_lapse = -2.0 * lapse * (trace_k - 2.0 * theta)
    rhs_theta = lapse * (trace_k * trace_k / 3.0 - 0.5 * square) - 0.04 * lapse * theta
    rhs_shift = [0.75 * state[22 + i] for i in range(3)]
    rhs_driver = [rhs_gamma[i] - 2.0 * state[22 + i] for i in range(3)]
    pieces = (
        [rhs_chi]
        + rhs_metric
        + [rhs_k]
        + rhs_curv
        + rhs_gamma
        + [rhs_lapse, rhs_theta]
        + rhs_shift
        + rhs_driver
    )
    rhs = jnp.stack(pieces, axis=0)
    advect = state[19][None] * first[0] + state[20][None] * first[1] + state[21][None] * first[2]
    return rhs + advect + sigma * smooth


def edge_copy(block, axis, start):
    edge = lax.slice_in_dim(block, start, start + 1, axis=axis)
    return jnp.concatenate([edge, edge, edge], axis=axis)


def body(section_fields, base_fields, flags):
    rows_z, rows_x, rows_y = (
        section_fields.shape[1],
        section_fields.shape[2],
        section_fields.shape[3],
    )
    blocks_x = lax.axis_size("gx")
    blocks_y = lax.axis_size("gy")
    index_x = lax.axis_index("gx")
    index_y = lax.axis_index("gy")
    padded_z = with_halo(section_fields, (("gz", 1),), 3, True)
    sides = with_halo(section_fields, (("gx", 2), ("gy", 3)), 3, False)
    signs = jnp.array(SIGN_TABLE, dtype=jnp.float32)[:, None, None, None]
    rotated = section_fields[:, :, 2::-1, ::-1] * signs
    for bit in range(blocks_y.bit_length() - 1):
        rotated = from_partner(rotated, "gy", bit)
    along_x = sides[:, :, :, 3 : 3 + rows_y]
    along_y = sides[:, :, 3 : 3 + rows_x, :]
    low_x = jnp.where(index_x == 0, rotated, along_x[:, :, :3])
    high_x = jnp.where(
        index_x == blocks_x - 1,
        edge_copy(section_fields, 2, rows_x - 1),
        along_x[:, :, rows_x + 3 :],
    )
    padded_x = jnp.concatenate([low_x, section_fields, high_x], axis=2)
    low_y = jnp.where(index_y == 0, edge_copy(section_fields, 3, 0), along_y[:, :, :, :3])
    high_y = jnp.where(
        index_y == blocks_y - 1,
        edge_copy(section_fields, 3, rows_y - 1),
        along_y[:, :, :, rows_y + 3 :],
    )
    padded_y = jnp.concatenate([low_y, section_fields, high_y], axis=3)
    diff_z = differences(padded_z, 1, rows_z)
    diff_x = differences(padded_x, 2, rows_x)
    diff_y = differences(padded_y, 3, rows_y)
    first = (diff_x[0], diff_y[0], diff_z[0])
    second = (diff_x[1], diff_y[1], diff_z[1])
    smooth = diff_x[2] + diff_y[2] + diff_z[2]
    sigma = 0.05 + 0.75 * flags[0, 0].astype(jnp.float32)
    rhs = evolve(section_fields, first, second, smooth, sigma)
    return base_fields + 0.25 * rhs


def solution(mesh):
    return jax.shard_map(
        body,
        mesh=mesh,
        in_specs=(P(None, "gz", "gx", "gy"), P(None, "gz", "gx", "gy"), P("gx", "gy")),
        out_specs=P(None, "gz", "gx", "gy"),
        check_vma=False,
    )
```

profile of v0, /device:TPU:224, one launch (start us, length us, event | category | flops | bytes accessed | tf_op | source)
XLA Modules:
  0.0 170.4 jit_solution(3062266162696874000)
XLA Ops:
  0.0 1.6 fusion.65
  1.6 0.7 copy.40
  2.3 3.0 %collective-permute-start.4 = (f32[25,8,3,128]{3,1,2,0:T(8,128)}, f32[25,8,3,128]{3,1,2,0:T(8,128)}, u32[]{:S(2)}, u32[]{:S(2)}) collective-permute-start(f32[25,8,3,128]{3,1,2,0:T(8,128)} %copy.40), channel_id=1, source_target_pairs={{16,0},{32,16},{48,32},{64,48},{80,64},{96,80},{112,96},{128,112},... | collective-permute-start | bytes 921608 | tf_op jit(solution)/shard_map/ppermute | solution.py:44
  5.4 0.0 copy-start
  5.4 0.8 copy.41
  6.1 5.2 %collective-permute-start.3 = (f32[25,8,3,128]{3,1,2,0:T(8,128)}, f32[25,8,3,128]{3,1,2,0:T(8,128)}, u32[]{:S(2)}, u32[]{:S(2)}) collective-permute-start(f32[25,8,3,128]{3,1,2,0:T(8,128)} %copy.41), channel_id=1, source_target_pairs={{0,16},{16,32},{32,48},{48,64},{64,80},{80,96},{96,112},{112,128},... | collective-permute-start | bytes 921608 | tf_op jit(solution)/shard_map/ppermute | solution.py:43
  11.3 3.3 %fusion.66 = (f32[25,3,32,128]{3,2,1,0:T(8,128)}, f32[25,3,32,128]{3,2,1,0:T(8,128)}) fusion(f32[25,8,32,128]{3,2,1,0:T(8,128)} %param.4), kind=kLoop, calls=%fused_computation.145 | loop fusion | bytes 4915200 | tf_op jit(solution)/shard_map/slice | solution.py:41
  14.6 3.0 %collective-permute-start.7 = (f32[25,3,32,128]{3,2,1,0:T(8,128)}, f32[25,3,32,128]{3,2,1,0:T(8,128)}, u32[]{:S(2)}, u32[]{:S(2)}) collective-permute-start(f32[25,3,32,128]{3,2,1,0:T(8,128)} %get-tuple-element.37), channel_id=1, source_target_pairs={{0,1},{1,0},{2,3},{3,2},{4,5},{5,4},{6,7},{7,6},{8,9},{9,8},{10,11... | collective-permute-start | bytes 3686408 | tf_op jit(solution)/shard_map/ppermute | solution.py:43
  17.6 0.5 collective-permute-start.8
  18.2 1.8 %rev.3 = f32[25,8,3,128]{3,1,2,0:T(8,128)} reverse(f32[25,8,3,128]{3,1,2,0:T(8,128)} %copy.40), dimensions={2,3} | reverse | bytes 614400 | tf_op jit(solution)/shard_map/rev | solution.py:162
  20.0 1.8 %broadcast_multiply_fusion = f32[25,8,3,128]{3,1,2,0:T(8,128)} fusion(f32[25,8,3,128]{3,1,2,0:T(8,128)} %rev.3, f32[25]{0:T(128)S(1)} %copy-done.8), kind=kLoop, calls=%fused_computation.55 | loop fusion | flops 76800 | bytes 614500 | tf_op jit(solution)/shard_map/mul | solution.py:162
  21.8 0.0 collective-permute-start
  21.8 4.1 %fusion.64 = (f32[25,8,32,1]{3,2,1,0:T(8,128)}, f32[25,8,32,1]{3,2,1,0:T(8,128)}) fusion(f32[25,8,32,128]{3,2,1,0:T(8,128)S(1)} %copy-done), kind=kLoop, calls=%fused_computation.143 | loop fusion | bytes 102400 | tf_op jit(solution)/shard_map/slice | solution.py:145
  25.8 7.5 %copy.35 = f32[25,8,32,128]{2,1,3,0:T(8,128)} copy(f32[25,8,32,128]{3,2,1,0:T(8,128)S(1)} %copy-done) | data formatting | bytes 6553600 | tf_op args[0]
  33.4 0.1 slice.191
  33.5 3.4 %copy.42 = f32[25,8,32,1]{2,1,0,3:T(8,128)} copy(f32[25,8,32,1]{3,2,1,0:T(8,128)} %get-tuple-element.33) | data formatting | bytes 51200
  36.9 2.9 %copy.43 = f32[25,8,32,1]{2,1,0,3:T(8,128)S(1)} copy(f32[25,8,32,1]{3,2,1,0:T(8,128)} %get-tuple-element.34) | data formatting | bytes 51200
  40.5 0.0 collective-permute-done.4
  40.5 7.7 %copy.36 = f32[25,8,3,128]{2,1,3,0:T(8,128)} copy(f32[25,8,3,128]{3,1,2,0:T(8,128)} %collective-permute-done.4) | data formatting | bytes 614400 | tf_op jit(solution)/shard_map/ppermute | solution.py:44
  48.2 7.6 %copy.34 = f32[25,8,3,128]{2,1,3,0:T(8,128)} copy(f32[25,8,3,128]{3,1,2,0:T(8,128)} %collective-permute-done.3) | data formatting | bytes 614400 | tf_op jit(solution)/shard_map/ppermute | solution.py:43
  55.8 1.6 collective-permute-start.1
  57.4 2.5 %pad_maximum_fusion.5 = (f32[25,8,38,3]{2,1,3,0:T(8,128)S(1)}, f32[25,8,38,3]{2,1,3,0:T(8,128)}) fusion(f32[25,8,3,128]{2,1,3,0:T(8,128)} %copy.36, f32[25,8,32,128]{2,1,3,0:T(8,128)} %copy.35, f32[25,8,3,128]{2,1,3,0:T(8,128)} %copy.34), kind=kLoop, calls=%fused_computation.53 | loop fusion | flops 91200 | bytes 4073600 | tf_op jit(solution)/shard_map/slice | solution.py:41
  59.9 2.1 %collective-permute-start.5 = (f32[25,8,38,3]{2,1,3,0:T(8,128)S(1)}, f32[25,8,38,3]{2,1,3,0:T(8,128)S(1)}, u32[]{:S(2)}, u32[]{:S(2)}) collective-permute-start(f32[25,8,38,3]{2,1,3,0:T(8,128)S(1)} %get-tuple-element.16), channel_id=1, source_target_pairs={{0,2},{2,4},{4,6},{6,8},{8,10},{10,12},{12,14},{1,3},{3,5},{5,7},{... | collective-permute-start | bytes 273608 | tf_op jit(solution)/shard_map/ppermute | solution.py:43
  62.0 1.3 collective-permute-start.6
  63.3 1.7 %broadcast_select_fusion = f32[25,8,3,128]{3,1,2,0:T(8,128)} fusion(f32[25,8,3,128]{3,1,2,0:T(8,128)} %collective-permute-done.4, f32[25,8,128]{2,1,0:T(8,128)S(1)} %bitcast.10, pred[]{:T(512)S(6)} %eq.13), kind=kLoop, calls=%fused_computation.54 | loop fusion | flops 76800 | bytes 716801 | tf_op jit(solution)/shard_map/jit(_where)/select_n | solution.py:168
  65.1 0.7 collective-permute-done.1
  65.8 4.3 %collective-permute-start.2 = (f32[25,8,3,128]{3,1,2,0:T(8,128)}, f32[25,8,3,128]{3,1,2,0:T(8,128)}, u32[]{:S(2)}, u32[]{:S(2)}) collective-permute-start(f32[25,8,3,128]{3,1,2,0:T(8,128)} %collective-permute-done.1), channel_id=1, source_target_pairs={{0,8},{8,0},{2,10},{10,2},{4,12},{12,4},{6,14},{14,6},{1,9},{9,1},... | collective-permute-start | bytes 921608 | tf_op jit(solution)/shard_map/ppermute | solution.py:56
  70.1 0.9 slice_select_fusion.1
  71.0 3.4 %copy.37 = f32[25,8,32,3]{3,2,1,0:T(8,128)} copy(f32[25,8,32,3]{2,1,3,0:T(8,128)} %slice_select_fusion.1) | data formatting | bytes 153600 | tf_op jit(solution)/shard_map/jit(_where)/select_n | solution.py:174
  74.4 1.8 %slice_select_fusion = f32[25,8,32,3]{2,1,3,0:T(8,128)} fusion(f32[25,8,38,3]{2,1,3,0:T(8,128)} %collective-permute-done.6, f32[25,8,32]{2,1,0:T(8,128)S(1)} %bitcast.11, pred[]{:T(512)S(6)} %eq.15), kind=kLoop, calls=%fused_computation.49 | loop fusion | flops 19200 | bytes 179201 | tf_op jit(solution)/shard_map/jit(_where)/select_n | solution.py:175
  76.2 3.5 %copy.39 = f32[25,8,32,3]{3,2,1,0:T(8,128)} copy(f32[25,8,32,3]{2,1,3,0:T(8,128)} %slice_select_fusion) | data formatting | bytes 153600 | tf_op jit(solution)/shard_map/jit(_where)/select_n | solution.py:175
  79.7 1.2 broadcast_select_fusion.1
  80.9 0.9 copy.31
  81.7 2.4 %constant_dynamic-update-slice_fusion.2 = f32[25,11,32,128]{3,2,1,0:T(8,128)} fusion(f32[25,3,32,128]{3,2,1,0:T(8,128)} %collective-permute-done.7), kind=kLoop, calls=%fused_computation.137 | loop fusion | bytes 2457600
  84.2 18.2 %subtract_multiply_fusion.1 = (f32[25,8,32,128]{3,2,1,0:T(8,128)}, f32[25,8,32,128]{3,2,1,0:T(8,128)}, f32[25,11,32,128]{3,2,1,0:T(8,128)}, f32[25,11,32,128]{3,2,1,0:T(8,128)}, f32[25,8,35,128]{3,2,1,0:T(8,128)}) fusion(f32[25,8,32,128]{3,2,1,0:T(8,128)S(1)} %copy-done, f32[25,8,32,3]{3,2,1,0:T(8,128)S(1)} %copy-done.1, f32[25,8,32,3]{3,2,1,0:T(8,128)} %copy.39, ...), kind=kLoop, calls=%fused_computation.40 | loop fusion | flops 18841600 | bytes 23014400 | tf_op jit(solution)/shard_map/div | solution.py:70
  102.4 0.9 copy_dynamic-update-slice_fusion
  103.4 2.4 %constant_dynamic-update-slice_fusion.3 = f32[25,11,32,128]{3,2,1,0:T(8,128)} fusion(f32[25,11,32,128]{3,2,1,0:T(8,128)} %get-tuple-element.30, f32[25,3,32,128]{3,2,1,0:T(8,128)} %collective-permute-done.8), kind=kLoop, calls=%fused_computation.138 | loop fusion | bytes 2457600 | tf_op jit(solution)/shard_map/concatenate | solution.py:45
  105.8 13.0 %subtract_multiply_fusion.2 = (f32[25,8,32,128]{3,2,1,0:T(8,128)}, f32[25,8,32,128]{3,2,1,0:T(8,128)}, f32[25,8,32,128]{3,2,1,0:T(8,128)}, f32[25,8,32,128]{3,2,1,0:T(8,128)}) fusion(f32[25,8,35,128]{3,2,1,0:T(8,128)} %copy_dynamic-update-slice_fusion, f32[25,8,32,128]{3,2,1,0:T(8,128)S(1)} %copy-done, f32[25,8,3,128]{3,2,1,0:T(4,128)} %copy.31, ...), kind=kLoop, calls=%fused_computation.41 | loop fusion | flops 27033600 | bytes 36352000 | tf_op jit(solution)/shard_map/div | solution.py:70
  118.8 1.9 %multiply_dynamic-update-slice_fusion.4 = (f32[25,8,32,128]{3,2,1,0:T(8,128)}, f32[1,8,32,128]{3,2,1,0:T(8,128)S(1)}) fusion(f32[25,8,32,128]{3,2,1,0:T(8,128)S(1)} %copy-done, f32[25,8,32,128]{3,2,1,0:T(8,128)} %get-tuple-element.28, f32[25,8,32,128]{3,2,1,0:T(8,128)} %get-tuple-element.19, f32[25,8,32,128]{3,2,1,0:T(8,128)} %get-tuple-element.23), kind=kLoop, calls=%fused_computation.133 | loop fusion | flops 196607 | bytes 1048576
  120.7 1.9 %fusion.60 = f32[25,8,32,128]{3,2,1,0:T(8,128)} fusion(f32[25,8,32,128]{3,2,1,0:T(8,128)} %get-tuple-element.14, f32[1,8,32,128]{3,2,1,0:T(8,128)S(1)} %get-tuple-element.15, f32[25,8,32,128]{3,2,1,0:T(8,128)S(1)} %copy-done, f32[25,8,32,128]{3,2,1,0:T(8,128)} %get-tuple-element.23), kind=kLoop, calls=%fused_computation.110 | loop fusion | flops 458752 | bytes 1310720
  122.6 2.0 %subtract_dynamic-update-slice_fusion.8 = f32[25,8,32,128]{3,2,1,0:T(8,128)} fusion(f32[25,8,32,128]{3,2,1,0:T(8,128)} %fusion.60, f32[1,8,32,128]{3,2,1,0:T(8,128)S(1)} %get-tuple-element.15, f32[25,8,32,128]{3,2,1,0:T(8,128)S(1)} %copy-done, f32[25,8,32,128]{3,2,1,0:T(8,128)} %get-tuple-element.19, f32[25,8,32,128]{3,2,1,0:T(8,128)} %get-tuple-element.23), kind=kLoop, calls=%fused_computation.132 | loop fusion | flops 557056 | bytes 1966080
  124.7 2.0 %subtract_dynamic-update-slice_fusion.7 = f32[25,8,32,128]{3,2,1,0:T(8,128)} fusion(f32[25,8,32,128]{3,2,1,0:T(8,128)} %subtract_dynamic-update-slice_fusion.8, f32[1,8,32,128]{3,2,1,0:T(8,128)S(1)} %get-tuple-element.15, f32[25,8,32,128]{3,2,1,0:T(8,128)S(1)} %copy-done, f32[25,8,32,128]{3,2,1,0:T(8,128)} %get-tuple-element.28, ...), kind=kLoop, calls=%fused_computation.131 | loop fusion | flops 557056 | bytes 1966080
  126.7 0.8 fusion.57
  127.5 0.9 subtract_dynamic-update-slice_fusion.6
  128.3 0.8 fusion.54
  129.1 1.8 %add_dynamic-update-slice_fusion = (f32[25,8,32,128]{3,2,1,0:T(8,128)}, f32[1,8,32,128]{3,2,1,0:T(8,128)S(1)}, f32[1,8,32,128]{3,2,1,0:T(8,128)S(1)}) fusion(f32[25,8,32,128]{3,2,1,0:T(8,128)} %fusion.54, f32[25,8,32,128]{3,2,1,0:T(8,128)S(1)} %copy-done, f32[25,8,32,128]{3,2,1,0:T(8,128)} %get-tuple-element.29, f32[25,8,32,128]{3,2,1,0:T(8,128)} %get-tuple-element.18, ...), kind=kLoop, calls=%fused_computation.125 | loop fusion | flops 753664 | bytes 1966080
  131.0 1.7 %fusion.51 = f32[25,8,32,128]{3,2,1,0:T(8,128)} fusion(f32[25,8,32,128]{3,2,1,0:T(8,128)} %get-tuple-element.11, f32[1,8,32,128]{3,2,1,0:T(8,128)S(1)} %get-tuple-element.15, f32[25,8,32,128]{3,2,1,0:T(8,128)} %get-tuple-element.22, f32[1,8,32,128]{3,2,1,0:T(8,128)S(1)} %get-tuple-element.12, f32[25,8,32,128]{3,2,1,0:T(8,128)S(1)} %copy-done, ...), kind=kLoop, calls=%fused_computation.95 | loop fusion | flops 819200 | bytes 1703936
  132.7 0.9 fusion.47
  133.6 0.8 subtract_dynamic-update-slice_fusion.5
  134.4 1.7 %fusion.41 = f32[25,8,32,128]{3,2,1,0:T(8,128)} fusion(f32[25,8,32,128]{3,2,1,0:T(8,128)} %subtract_dynamic-update-slice_fusion.5, f32[1,8,32,128]{3,2,1,0:T(8,128)S(1)} %get-tuple-element.15, f32[25,8,32,128]{3,2,1,0:T(8,128)} %get-tuple-element.18, f32[1,8,32,128]{3,2,1,0:T(8,128)S(1)} %get-tuple-element.12, f32[25,8,32,128]{3,2,1,0:T(8,128)S(1)} %copy-done, ...), kind=kLoop, calls=%fused_computation.82 | loop fusion | flops 819200 | bytes 1703936
  136.1 0.9 subtract_dynamic-update-slice_fusion.4
  137.0 1.7 %fusion.37 = f32[25,8,32,128]{3,2,1,0:T(8,128)} fusion(f32[25,8,32,128]{3,2,1,0:T(8,128)} %subtract_dynamic-update-slice_fusion.4, f32[1,8,32,128]{3,2,1,0:T(8,128)S(1)} %get-tuple-element.15, f32[25,8,32,128]{3,2,1,0:T(8,128)} %get-tuple-element.29, f32[1,8,32,128]{3,2,1,0:T(8,128)S(1)} %get-tuple-element.12, f32[25,8,32,128]{3,2,1,0:T(8,128)S(1)} %copy-done, ...), kind=kLoop, calls=%fused_computation.76 | loop fusion | flops 819200 | bytes 1703936
  138.7 1.9 %constant_dynamic-update-slice_fusion.7 = (f32[25,8,32,128]{3,2,1,0:T(8,128)}, f32[1,8,32,128]{3,2,1,0:T(8,128)S(1)}) fusion(f32[25,8,32,128]{3,2,1,0:T(8,128)} %fusion.37, f32[25,8,32,128]{3,2,1,0:T(8,128)S(1)} %copy-done.4, f32[25,8,32,128]{3,2,1,0:T(8,128)S(1)} %copy-done, f32[25,8,32,128]{3,2,1,0:T(8,128)S(1)} %copy-done.3, ...), kind=kLoop, calls=%fused_computation.142 | loop fusion | flops 589824 | bytes 2359296
  140.6 1.9 %constant_dynamic-update-slice_fusion.6 = (f32[25,8,32,128]{3,2,1,0:T(8,128)}, f32[1,8,32,128]{3,2,1,0:T(8,128)S(1)}) fusion(f32[25,8,32,128]{3,2,1,0:T(8,128)} %get-tuple-element.9, f32[25,8,32,128]{3,2,1,0:T(8,128)S(1)} %copy-done.4, f32[25,8,32,128]{3,2,1,0:T(8,128)S(1)} %copy-done, f32[25,8,32,128]{3,2,1,0:T(8,128)S(1)} %copy-done.3, ...), kind=kLoop, calls=%fused_computation.141 | loop fusion | flops 589824 | bytes 2359296
  142.5 2.1 %constant_dynamic-update-slice_fusion.5 = (f32[25,8,32,128]{3,2,1,0:T(8,128)}, f32[1,8,32,128]{3,2,1,0:T(8,128)S(1)}) fusion(f32[25,8,32,128]{3,2,1,0:T(8,128)} %get-tuple-element.7, f32[25,8,32,128]{3,2,1,0:T(8,128)S(1)} %copy-done.4, f32[25,8,32,128]{3,2,1,0:T(8,128)S(1)} %copy-done.3, f32[25,8,32,128]{3,2,1,0:T(8,128)S(1)} %copy-done, ...), kind=kLoop, calls=%fused_computation.140 | loop fusion | flops 589824 | bytes 2359296
  144.6 0.7 multiply_dynamic-update-slice_fusion.3
  145.2 0.7 subtract_dynamic-update-slice_fusion.3
  145.9 0.7 multiply_dynamic-update-slice_fusion.2
  146.6 0.7 multiply_dynamic-update-slice_fusion.1
  147.2 0.8 multiply_bitcast_fusion.2
  148.0 0.7 subtract_dynamic-update-slice_fusion.2
  148.7 0.7 subtract_dynamic-update-slice_fusion.1
  149.3 0.7 subtract_dynamic-update-slice_fusion
  150.0 20.2 %fusion.13 = f32[25,8,32,128]{3,2,1,0:T(8,128)} fusion(f32[25,8,32,128]{3,2,1,0:T(8,128)} %param.5, f32[25,11,32,128]{3,2,1,0:T(8,128)} %constant_dynamic-update-slice_fusion.3, f32[25,11,32,128]{3,2,1,0:T(8,128)} %get-tuple-element.31, f32[25,8,32,3]{3,2,1,0:T(8,128)} %copy.39, f32[25,8,32,128]{3,2,1,0:T(8,128)S(1)} %copy-done, ...), kind=kLoop, calls=%fused_computation.26 | loop fusion | flops 49971200 | bytes 43452420 | tf_op jit(solution)/shard_map/add | solution.py:189
  (24 shorter events, 0.1 us)
Async XLA Ops:
  2.3 17.7 %copy-start.8 = (f32[25]{0:T(128)S(1)}, f32[25]{0:T(128)}, u32[]{:S(2)}) copy-start(f32[25]{0:T(128)} %constant.69.clone) | copy-start | bytes 304
  2.3 38.1 %collective-permute-start.4 = (f32[25,8,3,128]{3,1,2,0:T(8,128)}, f32[25,8,3,128]{3,1,2,0:T(8,128)}, u32[]{:S(2)}, u32[]{:S(2)}) collective-permute-start(f32[25,8,3,128]{3,1,2,0:T(8,128)} %copy.40), channel_id=1, source_target_pairs={{16,0},{32,16},{48,32},{64,48},{80,64},{96,80},{112,96},{128,112},... | collective-permute-start | bytes 921608 | tf_op jit(solution)/shard_map/ppermute | solution.py:44
  5.4 16.4 %copy-start = (f32[25,8,32,128]{3,2,1,0:T(8,128)S(1)}, f32[25,8,32,128]{3,2,1,0:T(8,128)}, u32[]{:S(2)}) copy-start(f32[25,8,32,128]{3,2,1,0:T(8,128)} %param.4) | copy-start | bytes 9830404
  6.1 42.0 %collective-permute-start.3 = (f32[25,8,3,128]{3,1,2,0:T(8,128)}, f32[25,8,3,128]{3,1,2,0:T(8,128)}, u32[]{:S(2)}, u32[]{:S(2)}) collective-permute-start(f32[25,8,3,128]{3,1,2,0:T(8,128)} %copy.41), channel_id=1, source_target_pairs={{0,16},{16,32},{32,48},{48,64},{64,80},{80,96},{96,112},{112,128},... | collective-permute-start | bytes 921608 | tf_op jit(solution)/shard_map/ppermute | solution.py:43
  14.6 67.1 %collective-permute-start.7 = (f32[25,3,32,128]{3,2,1,0:T(8,128)}, f32[25,3,32,128]{3,2,1,0:T(8,128)}, u32[]{:S(2)}, u32[]{:S(2)}) collective-permute-start(f32[25,3,32,128]{3,2,1,0:T(8,128)} %get-tuple-element.37), channel_id=1, source_target_pairs={{0,1},{1,0},{2,3},{3,2},{4,5},{5,4},{6,7},{7,6},{8,9},{9,8},{10,11... | collective-permute-start | bytes 3686408 | tf_op jit(solution)/shard_map/ppermute | solution.py:43
  17.6 85.7 %collective-permute-start.8 = (f32[25,3,32,128]{3,2,1,0:T(8,128)}, f32[25,3,32,128]{3,2,1,0:T(8,128)}, u32[]{:S(2)}, u32[]{:S(2)}) collective-permute-start(f32[25,3,32,128]{3,2,1,0:T(8,128)} %get-tuple-element.38), channel_id=1, source_target_pairs={{1,0},{0,1},{3,2},{2,3},{5,4},{4,5},{7,6},{6,7},{9,8},{8,9},{11,10... | collective-permute-start | bytes 3686408 | tf_op jit(solution)/shard_map/ppermute | solution.py:44
  21.8 34.0 %collective-permute-start = (f32[25,8,3,128]{3,1,2,0:T(8,128)}, f32[25,8,3,128]{3,1,2,0:T(8,128)}, u32[]{:S(2)}, u32[]{:S(2)}) collective-permute-start(f32[25,8,3,128]{3,1,2,0:T(8,128)} %broadcast_multiply_fusion), channel_id=1, source_target_pairs={{0,2},{2,0},{4,6},{6,4},{8,10},{10,8},{12,14},{14,12},{1,3},{3,1},... | collective-permute-start | bytes 921608 | tf_op jit(solution)/shard_map/ppermute | solution.py:56
  55.8 14.3 %copy-start.7 = (f32[25,8,32,1]{2,1,0,3:T(8,128)S(1)}, f32[25,8,32,1]{2,1,0,3:T(8,128)}, u32[]{:S(2)}) copy-start(f32[25,8,32,1]{2,1,0,3:T(8,128)} %copy.42) | copy-start | bytes 76804
  55.8 10.0 %collective-permute-start.1 = (f32[25,8,3,128]{3,1,2,0:T(8,128)}, f32[25,8,3,128]{3,1,2,0:T(8,128)}, u32[]{:S(2)}, u32[]{:S(2)}) collective-permute-start(f32[25,8,3,128]{3,1,2,0:T(8,128)} %collective-permute-done), channel_id=1, source_target_pairs={{0,4},{4,0},{2,6},{6,2},{8,12},{12,8},{10,14},{14,10},{1,5},{5,1},... | collective-permute-start | bytes 921608 | tf_op jit(solution)/shard_map/ppermute | solution.py:56
  59.9 10.2 %collective-permute-start.5 = (f32[25,8,38,3]{2,1,3,0:T(8,128)S(1)}, f32[25,8,38,3]{2,1,3,0:T(8,128)S(1)}, u32[]{:S(2)}, u32[]{:S(2)}) collective-permute-start(f32[25,8,38,3]{2,1,3,0:T(8,128)S(1)} %get-tuple-element.16), channel_id=1, source_target_pairs={{0,2},{2,4},{4,6},{6,8},{8,10},{10,12},{12,14},{1,3},{3,5},{5,7},{... | collective-permute-start | bytes 273608 | tf_op jit(solution)/shard_map/ppermute | solution.py:43
  62.0 12.4 %collective-permute-start.6 = (f32[25,8,38,3]{2,1,3,0:T(8,128)}, f32[25,8,38,3]{2,1,3,0:T(8,128)}, u32[]{:S(2)}, u32[]{:S(2)}) collective-permute-start(f32[25,8,38,3]{2,1,3,0:T(8,128)} %get-tuple-element.17), channel_id=1, source_target_pairs={{2,0},{4,2},{6,4},{8,6},{10,8},{12,10},{14,12},{3,1},{5,3},{7,5},{... | collective-permute-start | bytes 273608 | tf_op jit(solution)/shard_map/ppermute | solution.py:44
  65.8 13.9 %collective-permute-start.2 = (f32[25,8,3,128]{3,1,2,0:T(8,128)}, f32[25,8,3,128]{3,1,2,0:T(8,128)}, u32[]{:S(2)}, u32[]{:S(2)}) collective-permute-start(f32[25,8,3,128]{3,1,2,0:T(8,128)} %collective-permute-done.1), channel_id=1, source_target_pairs={{0,8},{8,0},{2,10},{10,2},{4,12},{12,4},{6,14},{14,6},{1,9},{9,1},... | collective-permute-start | bytes 921608 | tf_op jit(solution)/shard_map/ppermute | solution.py:56
  79.7 4.5 %copy-start.1 = (f32[25,8,32,3]{3,2,1,0:T(8,128)S(1)}, f32[25,8,32,3]{3,2,1,0:T(8,128)}, u32[]{:S(2)}) copy-start(f32[25,8,32,3]{3,2,1,0:T(8,128)} %copy.37) | copy-start | bytes 230404
  84.2 18.2 %copy-start.6 = (f32[25,8,3,128]{3,1,2,0:T(8,128)S(1)}, f32[25,8,3,128]{3,1,2,0:T(8,128)}, u32[]{:S(2)}) copy-start(f32[25,8,3,128]{3,1,2,0:T(8,128)} %broadcast_select_fusion) | copy-start | bytes 921604
  118.8 7.9 %copy-start.3 = (f32[25,8,32,128]{3,2,1,0:T(8,128)S(1)}, f32[25,8,32,128]{3,2,1,0:T(8,128)}, u32[]{:S(2)}) copy-start(f32[25,8,32,128]{3,2,1,0:T(8,128)} %get-tuple-element.19) | copy-start | bytes 9830404
  120.7 6.8 %copy-start.4 = (f32[25,8,32,128]{3,2,1,0:T(8,128)S(1)}, f32[25,8,32,128]{3,2,1,0:T(8,128)}, u32[]{:S(2)}) copy-start(f32[25,8,32,128]{3,2,1,0:T(8,128)} %get-tuple-element.28) | copy-start | bytes 9830404
  126.7 4.2 %copy-start.5 = (f32[25,8,32,128]{3,2,1,0:T(8,128)S(1)}, f32[25,8,32,128]{3,2,1,0:T(8,128)}, u32[]{:S(2)}) copy-start(f32[25,8,32,128]{3,2,1,0:T(8,128)} %get-tuple-element.23) | copy-start | bytes 9830404
  142.5 7.5 %copy-start.2 = (f32[25,8,32,3]{3,2,1,0:T(8,128)S(1)}, f32[25,8,32,3]{3,2,1,0:T(8,128)}, u32[]{:S(2)}) copy-start(f32[25,8,32,3]{3,2,1,0:T(8,128)} %copy.37) | copy-start | bytes 230404
where the time goes:
time: 173 us; the launch traced here: 170 us
  other arithmetic  92.5 us (53%)
  local copies, waits for them, and re-layouts  55.1 us (32%)
  starting transfers between devices  21 us (12%)
    div x2, other arithmetic, differences(): (-shifted(-2) + 16.0 * shifted(-1) - 30.0 * centre + 16.0 * shifted(1) -...  31.3 us
    unnamed x23, other arithmetic  29.7 us
    add x1, other arithmetic, body(): return base_fields + 0.25 * rhs  20.2 us
    unnamed x24, local copies, waits for them, and re-layouts  17.8 us
    ppermute x3, starting transfers between devices, with_halo(): before = lax.ppermute(last, axis, up)  10.3 us
    ppermute x1, local copies, waits for them, and re-layouts, with_halo(): after = lax.ppermute(leading, axis, down)  7.71 us
    ppermute x1, local copies, waits for them, and re-layouts, with_halo(): before = lax.ppermute(last, axis, up)  7.59 us
    ppermute x3, starting transfers between devices, from_partner(): return lax.ppermute(block, axis, route)  5.89 us
  transfers between devices with their start and end apart: 9, of which 1 were waited for; matrix products, arithmetic and copies ran while one was open for 46% of the time, Pallas kernels for 0%

commit v1 on v0

v1 whole, which is shorter than its diff:
```python
import jax
import jax.numpy as jnp
from jax import lax
from jax.experimental import pallas as pl
from jax.experimental.pallas import tpu as pltpu
from jax.sharding import PartitionSpec as P

MESH = pl.DeviceIdType.MESH
FIELDS = 25
PAIRS = ((0, 0), (0, 1), (0, 2), (1, 1), (1, 2), (2, 2))
NEGATIVE = (3, 5, 10, 12, 14, 15, 19, 20, 22, 23)
FIRST = (17, 19, 20, 21)
REST = FIELDS - len(FIRST)
ROWS_Z, ROWS_X, ROWS_Y = 8, 32, 128
TILES = ROWS_X // 8
STEP = 0.25


def rest_field(p):
    return jnp.where(p < 17, p, jnp.where(p < 18, 18, p + 4))


def places():
    gx, gy, gz = lax.axis_index("gx"), lax.axis_index("gy"), lax.axis_index("gz")
    low = gx // 8
    across = (1 - low) * 8 + gx % 8
    plus = (across, gy, jnp.where(low == 1, 1 - gz, gz))
    minus = (across, gy, jnp.where(low == 0, 1 - gz, gz))
    partner = (gx, gy, 1 - gz)
    left = (gx, (gy + 7) % 8, gz)
    right = (gx, (gy + 1) % 8, gz)
    below = (jnp.where(gx == 0, 0, gx - 1), jnp.where(gx == 0, 7 - gy, gy), gz)
    above = (gx + 1, gy, gz)
    return gx, gy, plus, minus, partner, left, right, below, above


def remote(src, dst, send, recv, device):
    return pltpu.make_async_remote_copy(
        src_ref=src, dst_ref=dst, send_sem=send, recv_sem=recv, device_id=device, device_id_type=MESH
    )


def sym(i, j):
    return PAIRS.index((min(i, j), max(i, j)))


def evolve(s, d, dd):
    chi, trace, lapse, theta = s[0], s[7], s[17], s[18]
    g = lambda i, j: s[1 + sym(i, j)]
    a = lambda i, j: s[8 + sym(i, j)]
    grad = lambda k, j: d[19 + k][j]
    div = grad(0, 0) + grad(1, 1) + grad(2, 2)
    lap = dd[17][0] + dd[17][1] + dd[17][2]
    div23 = (2.0 / 3.0) * div
    square = (
        a(0, 0) * a(0, 0) + a(1, 1) * a(1, 1) + a(2, 2) * a(2, 2)
        + 2.0 * (a(0, 1) * a(0, 1) + a(0, 2) * a(0, 2) + a(1, 2) * a(1, 2))
    )
    out = {}
    out[0] = chi * ((2.0 / 3.0) * (lapse * trace) - div23)
    lapse2 = 2.0 * lapse
    for n, (i, j) in enumerate(PAIRS):
        if i == j:
            lie_g = 2.0 * sum(g(i, k) * grad(k, i) for k in range(3))
            lie_a = 2.0 * sum(a(i, k) * grad(k, i) for k in range(3))
        else:
            lie_g = sum(g(i, k) * grad(k, j) + g(j, k) * grad(k, i) for k in range(3))
            lie_a = sum(a(i, k) * grad(k, j) + a(j, k) * grad(k, i) for k in range(3))
        out[1 + n] = lie_g - lapse2 * a(i, j) - g(i, j) * div23
        quad = sum(a(i, k) * a(k, j) for k in range(3))
        term = lapse * (trace * a(i, j)) - lapse2 * quad + lie_a - a(i, j) * div23
        if i == j:
            term = term + chi * (lap * (1.0 / 3.0) - dd[17][i])
        out[8 + n] = term
    third = trace * trace * (1.0 / 3.0)
    out[7] = lapse * (square + third) - chi * lap
    for i in range(3):
        value = dd[19 + i][0] + dd[19 + i][1] + dd[19 + i][2]
        value = value - 2.0 * sum(a(i, j) * d[17][j] for j in range(3))
        value = value + s[14 + i] * div23
        value = value - sum(s[14 + j] * grad(i, j) for j in range(3))
        out[14 + i] = value
        out[22 + i] = value - 2.0 * s[22 + i]
        out[19 + i] = 0.75 * s[22 + i]
    out[17] = -lapse2 * (trace - 2.0 * theta)
    out[18] = lapse * (third - 0.5 * square) - 0.04 * (lapse * theta)
    return out


def kernel(
    sec, base, flag, signs, out,
    pad, acc, relay_p, relay_m, packed, from_left, from_right,
    load_sem, store_sem, z_send, z_recv, x_send, x_recv, y_send, y_recv,
):
    gx, gy, plus, minus, partner, left, right, below, above = places()
    inner = (slice(3, 11), slice(8, 40))
    load_s = pltpu.make_async_copy(sec, pad.at[:, 3:11, 8:40, :], load_sem.at[0])
    load_b = pltpu.make_async_copy(base, acc, load_sem.at[1])
    load_s.start()
    load_b.start()

    barrier = pltpu.get_barrier_semaphore()
    for device in (plus, minus, partner, left, right, below):
        pl.semaphore_signal(barrier, inc=1, device_id=device, device_id_type=MESH)

    @pl.when(gx < 15)
    def _():
        pl.semaphore_signal(barrier, inc=1, device_id=above, device_id_type=MESH)
        pl.semaphore_wait(barrier, 7)

    @pl.when(gx == 15)
    def _():
        pl.semaphore_wait(barrier, 6)

    def direct(n, f):
        return (
            remote(sec.at[f, 0:3], pad.at[f, 11:14, 8:40, :], z_send.at[0, n], z_recv.at[0, n], partner),
            remote(sec.at[f, 5:8], pad.at[f, 0:3, 8:40, :], z_send.at[1, n], z_recv.at[1, n], partner),
        )

    def hop1(p):
        f, n = rest_field(p), p + len(FIRST)
        return (
            remote(sec.at[f, 0:3], relay_p.at[p], z_send.at[0, n], z_recv.at[0, n], plus),
            remote(sec.at[f, 5:8], relay_m.at[p], z_send.at[1, n], z_recv.at[1, n], minus),
        )

    def hop2(p):
        f, n = rest_field(p), p + len(FIRST)
        return (
            remote(relay_p.at[p], pad.at[f, 11:14, 8:40, :], z_send.at[2, n], z_recv.at[2, n], plus),
            remote(relay_m.at[p], pad.at[f, 0:3, 8:40, :], z_send.at[3, n], z_recv.at[3, n], minus),
        )

    for n, f in enumerate(FIRST):
        for copy in direct(n, f):
            copy.start()

    to_above = remote(sec.at[:, :, 29:32, :], pad.at[:, 3:11, 5:8, :], x_send.at[3], x_recv.at[3], above)
    to_below = remote(sec.at[:, :, 0:3, :], pad.at[:, 3:11, 40:43, :], x_send.at[4], x_recv.at[4], below)
    to_mirror = [
        remote(sec.at[:, :, i:i + 1, :], pad.at[:, 3:11, 7 - i:8 - i, :], x_send.at[i], x_recv.at[i], below)
        for i in range(3)
    ]

    @pl.when(gx < 15)
    def _():
        to_above.start()

    @pl.when(gx > 0)
    def _():
        to_below.start()

    @pl.when(gx == 0)
    def _():
        for copy in to_mirror:
            copy.start()

    @pl.loop(0, REST)
    def _(p):
        for copy in hop1(p):
            copy.start()

    lane = lax.broadcasted_iota(jnp.int32, (8, 128), 1)
    load_s.wait()

    @pl.loop(0, ROWS_Z * TILES)
    def _(i):
        z, row = i // TILES, pl.multiple_of((i % TILES) * 8, 8)
        both = [jnp.zeros((8, 128), jnp.float32) for _ in range(2)]
        for f in range(FIELDS):
            half, slot = divmod(f, 16)
            tile = pltpu.roll(pad[f, z + 3, pl.ds(row + 8, 8), :], 3 + 8 * slot, 1)
            both[half] = jnp.where(lane >= 8 * slot, tile, both[half])
        for half in range(2):
            packed[half, z, pl.ds(row, 8), :] = both[half]

    to_left = remote(packed, from_right, y_send.at[0], y_recv.at[0], left)
    to_right = remote(packed, from_left, y_send.at[1], y_recv.at[1], right)
    to_left.start()
    to_right.start()

    @pl.when(gx > 0)
    def _():
        to_above.wait_recv()

    @pl.when(gx < 15)
    def _():
        to_below.wait_recv()

    @pl.when(gx == 0)
    def _():
        for copy in to_mirror:
            copy.wait_recv()
        turn = jnp.where(
            lax.broadcasted_iota(jnp.int32, (128, 128), 0) + lax.broadcasted_iota(jnp.int32, (128, 128), 1) == 127,
            1.0, 0.0,
        )

        @pl.loop(0, FIELDS)
        def _(f):
            rows = pad[f, 3:11, 0:8, :].reshape(64, 128)
            rows = jnp.dot(rows, turn, precision=lax.Precision.HIGHEST, preferred_element_type=jnp.float32)
            pad[f, 3:11, 0:8, :] = (rows * signs[f]).reshape(8, 8, 128)

    @pl.when(gx == 15)
    def _():
        @pl.loop(0, FIELDS)
        def _(f):
            edge = pad[f, 3:11, 39:40, :]
            pad[f, 3:11, 40:43, :] = jnp.broadcast_to(edge, (8, 3, 128))

    to_right.wait_recv()
    to_left.wait_recv()
    place = lane % 8

    @pl.loop(0, ROWS_Z * TILES)
    def _(i):
        z, row = i // TILES, pl.multiple_of((i % TILES) * 8, 8)
        for half in range(2):
            at = (half, z, pl.ds(row, 8), slice(None))
            own = packed[at]
            low = jnp.where(
                place == 0, pltpu.roll(own, 125, 1),
                jnp.where(place == 1, pltpu.roll(own, 126, 1), pltpu.roll(own, 127, 1)),
            )
            high = jnp.where(
                place == 3, pltpu.roll(own, 1, 1),
                jnp.where(place == 4, pltpu.roll(own, 2, 1), pltpu.roll(own, 3, 1)),
            )
            low = jnp.where(gy == 0, low, from_left[at])
            high = jnp.where(gy == 7, high, from_right[at])
            from_left[at] = jnp.where(place < 3, low, high)

    load_b.wait()
    for n, f in enumerate(FIRST):
        for copy in direct(n, f):
            copy.wait_recv()

    sigma = 0.05 + 0.75 * flag[0, 0].astype(jnp.float32)
    damp = sigma * (STEP / 64.0)

    @pl.loop(0, ROWS_Z * TILES)
    def _(i):
        z, row = i // TILES, pl.multiple_of((i % TILES) * 8, 8)

        @pl.when(i < REST)
        def _():
            for copy in hop1(i):
                copy.wait_recv()
            for copy in hop2(i):
                copy.start()

        here = (z + 3, pl.ds(row + 8, 8), slice(None))
        ghosts = [from_left[half, z, pl.ds(row, 8), :] for half in range(2)]
        s = [pad[(f,) + here] for f in range(FIELDS)]
        d, dd = {}, {}
        bx, by = s[19] * (STEP / 12.0), s[20] * (STEP / 12.0)
        partial = {}
        for f in FIRST + tuple(f for f in range(FIELDS) if f not in FIRST):
            c = s[f]
            half, slot = divmod(f, 16)
            ghost = pltpu.roll(ghosts[half], (128 - 8 * slot - 3) % 128, 1)
            up = [pad[f, z + 3, pl.ds(row + 8 + k, 8), :] for k in (1, 2, 3)]
            down = [pad[f, z + 3, pl.ds(row + 8 - k, 8), :] for k in (1, 2, 3)]
            right_ = [pltpu.roll(jnp.where(lane < k, ghost, c), 128 - k, 1) for k in (1, 2, 3)]
            left_ = [pltpu.roll(jnp.where(lane >= 128 - k, ghost, c), k, 1) for k in (1, 2, 3)]
            dx = 8.0 * (up[0] - down[0]) - (up[1] - down[1])
            dy = 8.0 * (right_[0] - left_[0]) - (right_[1] - left_[1])
            sx = [up[k] + down[k] for k in range(3)]
            sy = [right_[k] + left_[k] for k in range(3)]
            smooth = (sx[2] + sy[2]) - 6.0 * (sx[1] + sy[1]) + 15.0 * (sx[0] + sy[0]) - 40.0 * c
            partial[f] = bx * dx + by * dy + damp * smooth
            if f in FIRST:
                zs = {k: pad[f, z + 3 + k, pl.ds(row + 8, 8), :] for k in (-2, -1, 1, 2)}
                dz = 8.0 * (zs[1] - zs[-1]) - (zs[2] - zs[-2])
                sz = [zs[1] + zs[-1], zs[2] + zs[-2]]
                d[f] = [v * (1.0 / 12.0) for v in (dx, dy, dz)]
                dd[f] = [(16.0 * v[0] - v[1] - 30.0 * c) * (1.0 / 12.0) for v in (sx, sy, sz)]
        rhs = evolve(s, d, dd)
        for f in range(FIELDS):
            at = (f, z, pl.ds(row, 8), slice(None))
            acc[at] = acc[at] + (partial[f] + STEP * rhs[f])

    def along_z(f):
        @pl.loop(0, TILES)
        def _(t):
            row = pl.multiple_of(t * 8, 8)
            v = [pad[f, z, pl.ds(row + 8, 8), :] for z in range(14)]
            for z in range(8):
                w = v[z:z + 7]
                bz = pad[21, z + 3, pl.ds(row + 8, 8), :] * (STEP / 12.0)
                dz = 8.0 * (w[4] - w[2]) - (w[5] - w[1])
                smooth = (w[6] + w[0]) - 6.0 * (w[5] + w[1]) + 15.0 * (w[4] + w[2]) - 20.0 * w[3]
                at = (f, z, pl.ds(row, 8), slice(None))
                acc[at] = acc[at] + (bz * dz + damp * smooth)

    def store(f):
        return pltpu.make_async_copy(acc.at[f], out.at[f], store_sem.at[f])

    for f in FIRST:
        along_z(f)
        store(f).start()

    @pl.loop(0, REST)
    def _(p):
        f = rest_field(p)
        for copy in hop2(p):
            copy.wait_recv()
        along_z(f)
        store(f).start()

    for n, f in enumerate(FIRST):
        for copy in direct(n, f):
            copy.wait_send()

    @pl.loop(0, REST)
    def _(p):
        for copy in hop1(p):
            copy.wait_send()
        for copy in hop2(p):
            copy.wait_send()

    @pl.when(gx < 15)
    def _():
        to_above.wait_send()

    @pl.when(gx > 0)
    def _():
        to_below.wait_send()

    @pl.when(gx == 0)
    def _():
        for copy in to_mirror:
            copy.wait_send()

    to_left.wait_send()
    to_right.wait_send()

    @pl.loop(0, FIELDS)
    def _(f):
        store(f).wait()


def body(section_fields, base_fields, flags):
    f32 = jnp.float32
    signs = jnp.array([-1.0 if c in NEGATIVE else 1.0 for c in range(FIELDS)], f32)
    block = (FIELDS, ROWS_Z, ROWS_X, ROWS_Y)
    dma = pltpu.SemaphoreType.DMA
    return pl.pallas_call(
        kernel,
        out_shape=jax.ShapeDtypeStruct(block, f32),
        in_specs=[
            pl.BlockSpec(memory_space=pl.ANY),
            pl.BlockSpec(memory_space=pl.ANY),
            pl.BlockSpec(memory_space=pltpu.SMEM),
            pl.BlockSpec(memory_space=pltpu.SMEM),
        ],
        out_specs=pl.BlockSpec(memory_space=pl.ANY),
        scratch_shapes=[
            pltpu.VMEM((FIELDS, 14, 48, ROWS_Y), f32),
            pltpu.VMEM(block, f32),
            pltpu.VMEM((REST, 3, ROWS_X, ROWS_Y), f32),
            pltpu.VMEM((REST, 3, ROWS_X, ROWS_Y), f32),
            pltpu.VMEM((2, ROWS_Z, ROWS_X, ROWS_Y), f32),
            pltpu.VMEM((2, ROWS_Z, ROWS_X, ROWS_Y), f32),
            pltpu.VMEM((2, ROWS_Z, ROWS_X, ROWS_Y), f32),
            dma((2,)),
            dma((FIELDS,)),
            dma((4, FIELDS)),
            dma((4, FIELDS)),
            dma((5,)),
            dma((5,)),
            dma((2,)),
            dma((2,)),
        ],
        compiler_params=pltpu.CompilerParams(
            collective_id=0, has_side_effects=True, vmem_limit_bytes=48 * 2**20
        ),
        cost_estimate=pl.CostEstimate(flops=80_000_000, bytes_accessed=9_830_400, transcendentals=0),
        name="substep",
    )(section_fields, base_fields, flags, signs)


def solution(mesh):
    spec = P(None, "gz", "gx", "gy")
    return jax.shard_map(
        body, mesh=mesh, in_specs=(spec, spec, P("gx", "gy")), out_specs=spec, check_vma=False
    )
```

time: 173 us -> 71.1 us (0.41)
  other arithmetic: 92.5 us -> 0 us
  Pallas kernels: 0 us -> 66.9 us
  local copies, waits for them, and re-layouts: 55.1 us -> 2.36 us
  starting transfers between devices: 21 us -> 0 us
    pallas_call x0 -> x1, Pallas kernels: none -> 66.9 us  [body(): pl.pallas_call(kernel, out_shape=jax.ShapeDtypeStruct(block, f32), in_spe...]
    div x2 -> x0, other arithmetic: 31.3 us -> none  [differences(): (-shifted(-2) + 16.0 * shifted(-1) - 30.0 * centre + 16.0 * shifted(1) -...]
    unnamed x23 -> x0, other arithmetic: 29.7 us -> none
    ppermute x9 -> x0, starting transfers between devices: 21 us -> none  [the longest x3 10.3 us: with_halo(): before = lax.ppermute(last, axis, up)]
    add x1 -> x0, other arithmetic: 20.2 us -> none  [body(): return base_fields + 0.25 * rhs]
    unnamed x24 -> x3, local copies, waits for them, and re-layouts: 17.8 us -> 2.36 us
    ppermute x2 -> x0, local copies, waits for them, and re-layouts: 15.3 us -> none  [the longest x1 7.71 us: with_halo(): after = lax.ppermute(leading, axis, down)]
    slice x4 -> x0, local copies, waits for them, and re-layouts: 9.07 us -> none  [the longest x2 4.9 us: with_halo(): last = lax.slice_in_dim(array, length - width, length, axis=dim)]
  transfers between devices with their start and end apart: 9 -> 0, of which waited for: 1 -> 0; matrix products, arithmetic and copies ran while one was open for 46% -> 0% of each run, Pallas kernels for 0% -> 0%
where the time goes in v1:
time: 71.1 us; the launch traced here: 70 us
  Pallas kernels  66.9 us (94%)
  local copies, waits for them, and re-layouts  2.36 us (3%)
    pallas_call x1, Pallas kernels, body(): pl.pallas_call(kernel, out_shape=jax.ShapeDtypeStruct(block, f32), in_spe...  66.9 us
    unnamed x3, local copies, waits for them, and re-layouts  2.36 us

profile of v1, /device:TPU:224, one launch (start us, length us, event | category | flops | bytes accessed | tf_op | source)
XLA Modules:
  0.0 70.0 jit_solution(2980427630842397496)
XLA Ops:
  0.7 0.0 copy-start
  0.7 0.6 copy-done
  1.3 66.9 %substep.1 = f32[25,8,32,128]{3,2,1,0:T(8,128)S(1)} custom-call(f32[25,8,32,128]{3,2,1,0:T(8,128)} %sec.1, f32[25,8,32,128]{3,2,1,0:T(8,128)} %base.1, s32[1,1]{1,0:T(1,128)S(6)} %copy.6.flag, f32[25]{0:T(128)S(1)} %copy-done), custom_call_target="tpu_custom_call" | custom-call | flops 80000000 | bytes 9830400 | tf_op jit(solution)/shard_map/substep/pallas_call | solution.py:350
  68.3 1.7 %copy.7 = f32[25,8,32,128]{3,2,1,0:T(8,128)} copy(f32[25,8,32,128]{3,2,1,0:T(8,128)S(1)} %substep.1) | data formatting | bytes 6553600
Async XLA Ops:
  0.7 0.7 copy-start

commit v2 on v1

v2 whole, which is shorter than its diff:
```python
import jax
import jax.numpy as jnp
from jax import lax
from jax.experimental import pallas as pl
from jax.experimental.pallas import tpu as pltpu
from jax.sharding import PartitionSpec as P

MESH = pl.DeviceIdType.MESH
FIELDS = 25
PAIRS = ((0, 0), (0, 1), (0, 2), (1, 1), (1, 2), (2, 2))
NEGATIVE = (3, 5, 10, 12, 14, 15, 19, 20, 22, 23)
NEGATIVE_BITS = sum(1 << c for c in NEGATIVE)
FIRST = (17, 19, 20, 21)
EARLY = 8
ROWS_Z, ROWS_X, ROWS_Y = 8, 32, 128
TILES = ROWS_X // 8
STEP = 0.25


def field_at(n):
    rest = jnp.where(n < 21, n - 4, jnp.where(n < 22, 18, n))
    return jnp.where(n < 1, 17, jnp.where(n < 4, 18 + n, rest))


def remote(src, dst, send, recv, device):
    return pltpu.make_async_remote_copy(
        src_ref=src, dst_ref=dst, send_sem=send, recv_sem=recv, device_id=device, device_id_type=MESH
    )


def sym(i, j):
    return PAIRS.index((min(i, j), max(i, j)))


def evolve(s, d, dd):
    chi, trace, lapse, theta = s[0], s[7], s[17], s[18]
    g = lambda i, j: s[1 + sym(i, j)]
    a = lambda i, j: s[8 + sym(i, j)]
    grad = lambda k, j: d[19 + k][j]
    div = grad(0, 0) + grad(1, 1) + grad(2, 2)
    lap = dd[17][0] + dd[17][1] + dd[17][2]
    div23 = (2.0 / 3.0) * div
    square = (
        a(0, 0) * a(0, 0) + a(1, 1) * a(1, 1) + a(2, 2) * a(2, 2)
        + 2.0 * (a(0, 1) * a(0, 1) + a(0, 2) * a(0, 2) + a(1, 2) * a(1, 2))
    )
    out = {}
    out[0] = chi * ((2.0 / 3.0) * (lapse * trace) - div23)
    lapse2 = 2.0 * lapse
    for n, (i, j) in enumerate(PAIRS):
        if i == j:
            lie_g = 2.0 * sum(g(i, k) * grad(k, i) for k in range(3))
            lie_a = 2.0 * sum(a(i, k) * grad(k, i) for k in range(3))
        else:
            lie_g = sum(g(i, k) * grad(k, j) + g(j, k) * grad(k, i) for k in range(3))
            lie_a = sum(a(i, k) * grad(k, j) + a(j, k) * grad(k, i) for k in range(3))
        out[1 + n] = lie_g - lapse2 * a(i, j) - g(i, j) * div23
        quad = sum(a(i, k) * a(k, j) for k in range(3))
        term = lapse * (trace * a(i, j)) - lapse2 * quad + lie_a - a(i, j) * div23
        if i == j:
            term = term + chi * (lap * (1.0 / 3.0) - dd[17][i])
        out[8 + n] = term
    third = trace * trace * (1.0 / 3.0)
    out[7] = lapse * (square + third) - chi * lap
    for i in range(3):
        value = dd[19 + i][0] + dd[19 + i][1] + dd[19 + i][2]
        value = value - 2.0 * sum(a(i, j) * d[17][j] for j in range(3))
        value = value + s[14 + i] * div23
        value = value - sum(s[14 + j] * grad(i, j) for j in range(3))
        out[14 + i] = value
        out[22 + i] = value - 2.0 * s[22 + i]
        out[19 + i] = 0.75 * s[22 + i]
    out[17] = -lapse2 * (trace - 2.0 * theta)
    out[18] = lapse * (third - 0.5 * square) - 0.04 * (lapse * theta)
    return out


def kernel(
    sec, base, flag, out,
    pad, acc, cross, packed, from_left, from_right, flag_at,
    load_sem, store_sem, z_send, z_recv, x_send, x_recv, y_send, y_recv, leg_send, leg_recv, arrive_recv, hello,
):
    gx, gy, gz = lax.axis_index("gx"), lax.axis_index("gy"), lax.axis_index("gz")
    low, z, core = gx // 8, gx % 8, gy % 2
    partner = (gx, gy, 1 - gz)
    left, right = (gx, (gy + 7) % 8, gz), (gx, (gy + 1) % 8, gz)
    up, down = (gx + 1, gy, gz), (gx - 1, gy, gz)
    mirror = (0, 7 - gy, gz)
    last, first = (7, gy, gz), (8, gy, gz)
    is_last, is_first = gx == 7, gx == 8
    in_row = lambda half, q: (8 * half + q, gy, gz)

    load_s = pltpu.make_async_copy(sec, pad.at[:, 3:11, 8:40, :], load_sem.at[0])
    load_b = pltpu.make_async_copy(base, acc, load_sem.at[1])
    load_f = pltpu.make_async_copy(flag, flag_at, load_sem.at[2])
    load_s.start()
    load_b.start()
    load_f.start()

    barrier = pltpu.get_barrier_semaphore()

    def tell(semaphore, device):
        pl.semaphore_signal(semaphore, inc=1, device_id=device, device_id_type=MESH)

    tell(barrier, partner)

    @pl.when(core == 1)
    def _():
        tell(barrier, left)
        tell(barrier, right)

    @pl.when((core == 1) & (gx == 0))
    def _():
        tell(barrier, mirror)

    @pl.when(z < 7)
    def _():
        tell(barrier, up)

    @pl.when(gx != 7)
    def _():
        tell(barrier, last)

    @pl.when(is_first)
    def _():
        for q in range(8):
            tell(barrier, in_row(0, q))
            if q > 0:
                tell(barrier, in_row(1, q))

    expected = (
        1 + jnp.where(core == 0, 2, 0) + jnp.where((core == 0) & (gx == 0), 1, 0) + jnp.where(z > 0, 1, 0)
        + jnp.where(is_last, 15, 0) + jnp.where(is_first, 0, 1)
    )
    pl.semaphore_wait(barrier, expected)

    def z_copies(n):
        f = field_at(n)
        return (
            remote(sec.at[f, 0:3], pad.at[f, 11:14, 8:40, :], z_send.at[0, n], z_recv.at[0, n], partner),
            remote(sec.at[f, 5:8], pad.at[f, 0:3, 8:40, :], z_send.at[1, n], z_recv.at[1, n], partner),
        )

    @pl.loop(0, EARLY)
    def _(n):
        for copy in z_copies(n):
            copy.start()

    @pl.when(z > 0)
    def _():
        tell(hello.at[0], down)

    @pl.when(core == 0)
    def _():
        tell(hello.at[1], left)
        tell(hello.at[1], right)

    @pl.when((core == 0) & (gx == 0))
    def _():
        tell(hello.at[2], mirror)

    @pl.when(low == 0)
    def _():
        tell(hello.at[3], first)

    @pl.when(is_last)
    def _():
        for q in range(7):
            tell(hello.at[4], in_row(0, q))

    to_up = remote(sec.at[:, :, 29:32, :], pad.at[:, 3:11, 5:8, :], x_send.at[3], x_recv.at[3], up)
    to_down = remote(sec.at[:, :, 0:3, :], pad.at[:, 3:11, 40:43, :], x_send.at[4], x_recv.at[4], down)
    to_mirror = [
        remote(sec.at[:, :, i:i + 1, :], pad.at[:, 3:11, 7 - i:8 - i, :], x_send.at[i], x_recv.at[i], mirror)
        for i in range(3)
    ]

    def leg_out(half, q):
        rows = slice(29, 32) if half == 0 else slice(0, 3)
        own = q == 7 * half
        ghost = piece_ghost(half, q) if own else cross.at[:, 0:3, :]
        return remote(
            sec.at[:, q, rows, :], ghost, leg_send.at[q], arrive_recv.at[q] if own else leg_recv.at[0], in_row(1 - half, q)
        )

    def piece_ghost(half, q):
        return pad.at[:, 3 + q, 5:8, :] if half == 0 else pad.at[:, 3 + q, 40:43, :]

    def leg_in(half):
        return remote(
            cross.at[:, 0:3, :], piece_ghost(half, z), leg_send.at[8], arrive_recv.at[z], first if half == 0 else last
        )

    def piece(half, q):
        return remote(cross.at[:, 0:3, :], piece_ghost(half, q), leg_send.at[8], arrive_recv.at[q], first)

    @pl.when(z > 0)
    def _():
        to_down.start()

    @pl.when(is_last)
    def _():
        for q in range(8):
            leg_out(0, q).start()

    lane = lax.broadcasted_iota(jnp.int32, (8, 128), 1)
    load_s.wait()

    @pl.loop(0, ROWS_Z * TILES)
    def _(i):
        z, row = i // TILES, pl.multiple_of((i % TILES) * 8, 8)
        both = [jnp.zeros((8, 128), jnp.float32) for _ in range(2)]
        for f in range(FIELDS):
            half, slot = divmod(f, 16)
            tile = pltpu.roll(pad[f, z + 3, pl.ds(row + 8, 8), :], 3 + 8 * slot, 1)
            both[half] = jnp.where(lane >= 8 * slot, tile, both[half])
        for half in range(2):
            packed[half, z, pl.ds(row, 8), :] = both[half]

    to_left = remote(packed, from_right, y_send.at[0], y_recv.at[0], left)
    to_right = remote(packed, from_left, y_send.at[1], y_recv.at[1], right)

    @pl.when(core == 1)
    def _():
        pl.semaphore_wait(hello.at[1], 2)

    @pl.when(gy > 0)
    def _():
        to_left.start()

    @pl.when(gy < 7)
    def _():
        to_right.start()

    @pl.when(z < 7)
    def _():
        pl.semaphore_wait(hello.at[0], 1)
        to_up.start()

    @pl.when((core == 1) & (gx == 0))
    def _():
        pl.semaphore_wait(hello.at[2], 1)

    @pl.when(gx == 0)
    def _():
        for copy in to_mirror:
            copy.start()

    @pl.when(is_first)
    def _():
        pl.semaphore_wait(hello.at[3], 8)
        for q in range(8):
            leg_out(1, q).start()

    @pl.loop(EARLY, FIELDS)
    def _(n):
        for copy in z_copies(n):
            copy.start()

    @pl.when(gx < 7)
    def _():
        pl.semaphore_wait(hello.at[4], 1)
        leg_out(1, 0).wait_recv()
        leg_in(1).start()

    @pl.when(gx > 8)
    def _():
        leg_out(0, 1).wait_recv()
        leg_in(0).start()

    place = lax.broadcasted_iota(jnp.int32, (ROWS_X, 128), 1) % 8

    @pl.when(gy > 0)
    def _():
        to_right.wait_recv()

    @pl.when(gy < 7)
    def _():
        to_left.wait_recv()

    @pl.when(gy == 0)
    def _():
        @pl.loop(0, 2 * ROWS_Z)
        def _(i):
            own = packed[i // ROWS_Z, i % ROWS_Z]
            from_left[i // ROWS_Z, i % ROWS_Z] = jnp.where(
                place == 0, pltpu.roll(own, 125, 1),
                jnp.where(place == 1, pltpu.roll(own, 126, 1), pltpu.roll(own, 127, 1)),
            )

    @pl.when(gy == 7)
    def _():
        @pl.loop(0, 2 * ROWS_Z)
        def _(i):
            own = packed[i // ROWS_Z, i % ROWS_Z]
            from_right[i // ROWS_Z, i % ROWS_Z] = jnp.where(
                place == 3, pltpu.roll(own, 1, 1),
                jnp.where(place == 4, pltpu.roll(own, 2, 1), pltpu.roll(own, 3, 1)),
            )

    load_b.wait()
    load_f.wait()
    for n in range(len(FIRST)):
        for copy in z_copies(n):
            copy.wait_recv()

    sigma = 0.05 + 0.75 * flag_at[0, 0].astype(jnp.float32)
    damp = sigma * (STEP / 64.0)

    def tile(z, row):
        here = (z + 3, pl.ds(row + 8, 8), slice(None))
        ghosts = [
            jnp.where(lane % 8 < 3, from_left[half, z, pl.ds(row, 8), :], from_right[half, z, pl.ds(row, 8), :])
            for half in range(2)
        ]
        s = [pad[(f,) + here] for f in range(FIELDS)]
        d, dd = {}, {}
        bx, by = s[19] * (STEP / 12.0), s[20] * (STEP / 12.0)
        partial = {}
        for f in FIRST + tuple(f for f in range(FIELDS) if f not in FIRST):
            c = s[f]
            half, slot = divmod(f, 16)
            ghost = pltpu.roll(ghosts[half], (128 - 8 * slot - 3) % 128, 1)
            up = [pad[f, z + 3, pl.ds(row + 8 + k, 8), :] for k in (1, 2, 3)]
            down = [pad[f, z + 3, pl.ds(row + 8 - k, 8), :] for k in (1, 2, 3)]
            right_ = [pltpu.roll(jnp.where(lane < k, ghost, c), 128 - k, 1) for k in (1, 2, 3)]
            left_ = [pltpu.roll(jnp.where(lane >= 128 - k, ghost, c), k, 1) for k in (1, 2, 3)]
            dx = 8.0 * (up[0] - down[0]) - (up[1] - down[1])
            dy = 8.0 * (right_[0] - left_[0]) - (right_[1] - left_[1])
            sx = [up[k] + down[k] for k in range(3)]
            sy = [right_[k] + left_[k] for k in range(3)]
            smooth = (sx[2] + sy[2]) - 6.0 * (sx[1] + sy[1]) + 15.0 * (sx[0] + sy[0]) - 40.0 * c
            partial[f] = bx * dx + by * dy + damp * smooth
            if f in FIRST:
                zs = {k: pad[f, z + 3 + k, pl.ds(row + 8, 8), :] for k in (-2, -1, 1, 2)}
                dz = 8.0 * (zs[1] - zs[-1]) - (zs[2] - zs[-2])
                sz = [zs[1] + zs[-1], zs[2] + zs[-2]]
                d[f] = [v * (1.0 / 12.0) for v in (dx, dy, dz)]
                dd[f] = [(16.0 * v[0] - v[1] - 30.0 * c) * (1.0 / 12.0) for v in (sx, sy, sz)]
        rhs = evolve(s, d, dd)
        for f in range(FIELDS):
            at = (f, z, pl.ds(row, 8), slice(None))
            acc[at] = acc[at] + (partial[f] + STEP * rhs[f])

    @pl.loop(0, 2 * ROWS_Z)
    def _(i):
        tile(i // 2, pl.multiple_of(8 + 8 * (i % 2), 8))

    @pl.when(z > 0)
    def _():
        to_up.wait_recv()

    @pl.when(z < 7)
    def _():
        to_down.wait_recv()

    @pl.when(is_first)
    def _():
        for q in range(8):
            piece(0, q).wait_recv()

    @pl.when(is_last)
    def _():
        for q in range(8):
            piece(1, q).wait_recv()

    @pl.when(gx == 0)
    def _():
        for copy in to_mirror:
            copy.wait_recv()
        turn = jnp.where(
            lax.broadcasted_iota(jnp.int32, (128, 128), 0) + lax.broadcasted_iota(jnp.int32, (128, 128), 1) == 127,
            1.0, 0.0,
        )

        @pl.loop(0, FIELDS)
        def _(f):
            sign = (1 - 2 * ((NEGATIVE_BITS >> f) & 1)).astype(jnp.float32)
            rows = pad[f, 3:11, 0:8, :].reshape(64, 128)
            rows = jnp.dot(rows, turn, precision=lax.Precision.HIGHEST, preferred_element_type=jnp.float32)
            pad[f, 3:11, 0:8, :] = (rows * sign).reshape(8, 8, 128)

    @pl.when(gx == 15)
    def _():
        @pl.loop(0, FIELDS)
        def _(f):
            edge = pad[f, 3:11, 39:40, :]
            pad[f, 3:11, 40:43, :] = jnp.broadcast_to(edge, (8, 3, 128))

    @pl.loop(0, 2 * ROWS_Z)
    def _(i):
        tile(i // 2, pl.multiple_of(24 * (i % 2), 8))

    def along_z(f):
        @pl.loop(0, TILES)
        def _(t):
            row = pl.multiple_of(t * 8, 8)
            v = [pad[f, z, pl.ds(row + 8, 8), :] for z in range(14)]
            for z in range(8):
                w = v[z:z + 7]
                bz = pad[21, z + 3, pl.ds(row + 8, 8), :] * (STEP / 12.0)
                dz = 8.0 * (w[4] - w[2]) - (w[5] - w[1])
                smooth = (w[6] + w[0]) - 6.0 * (w[5] + w[1]) + 15.0 * (w[4] + w[2]) - 20.0 * w[3]
                at = (f, z, pl.ds(row, 8), slice(None))
                acc[at] = acc[at] + (bz * dz + damp * smooth)

    def store(f):
        return pltpu.make_async_copy(acc.at[f], out.at[f], store_sem.at[f])

    @pl.loop(0, FIELDS)
    def _(n):
        @pl.when(n >= len(FIRST))
        def _():
            for copy in z_copies(n):
                copy.wait_recv()

        f = field_at(n)
        along_z(f)
        store(f).start()

    @pl.loop(0, FIELDS)
    def _(n):
        for copy in z_copies(n):
            copy.wait_send()

    @pl.when(z > 0)
    def _():
        to_down.wait_send()

    @pl.when(z < 7)
    def _():
        to_up.wait_send()

    @pl.when(gx == 0)
    def _():
        for copy in to_mirror:
            copy.wait_send()

    @pl.when(is_last)
    def _():
        for q in range(8):
            leg_out(0, q).wait_send()

    @pl.when(is_first)
    def _():
        for q in range(8):
            leg_out(1, q).wait_send()

    @pl.when((gx != 7) & (gx != 8))
    def _():
        piece(0, 0).wait_send()

    @pl.when(gy > 0)
    def _():
        to_left.wait_send()

    @pl.when(gy < 7)
    def _():
        to_right.wait_send()

    @pl.loop(0, FIELDS)
    def _(f):
        store(f).wait()


def body(section_fields, base_fields, flags):
    f32 = jnp.float32
    block = (FIELDS, ROWS_Z, ROWS_X, ROWS_Y)
    dma = pltpu.SemaphoreType.DMA
    return pl.pallas_call(
        kernel,
        out_shape=jax.ShapeDtypeStruct(block, f32),
        in_specs=[
            pl.BlockSpec(memory_space=pl.ANY),
            pl.BlockSpec(memory_space=pl.ANY),
            pl.BlockSpec(memory_space=pl.ANY),
        ],
        out_specs=pl.BlockSpec(memory_space=pl.ANY),
        scratch_shapes=[
            pltpu.VMEM((FIELDS, 14, 48, ROWS_Y), f32),
            pltpu.VMEM(block, f32),
            pltpu.VMEM((FIELDS, 8, ROWS_Y), f32),
            pltpu.VMEM((2, ROWS_Z, ROWS_X, ROWS_Y), f32),
            pltpu.VMEM((2, ROWS_Z, ROWS_X, ROWS_Y), f32),
            pltpu.VMEM((2, ROWS_Z, ROWS_X, ROWS_Y), f32),
            pltpu.SMEM((1, 1), jnp.int32),
            dma((3,)),
            dma((FIELDS,)),
            dma((2, FIELDS)),
            dma((2, FIELDS)),
            dma((5,)),
            dma((5,)),
            dma((2,)),
            dma((2,)),
            dma((9,)),
            dma((1,)),
            dma((8,)),
            pltpu.SemaphoreType.REGULAR((5,)),
        ],
        compiler_params=pltpu.CompilerParams(
            collective_id=0, has_side_effects=True, vmem_limit_bytes=48 * 2**20
        ),
        cost_estimate=pl.CostEstimate(flops=80_000_000, bytes_accessed=9_830_400, transcendentals=0),
        name="substep",
    )(section_fields, base_fields, flags)


def solution(mesh):
    spec = P(None, "gz", "gx", "gy")
    return jax.shard_map(
        body, mesh=mesh, in_specs=(spec, spec, P("gx", "gy")), out_specs=spec, check_vma=False
    )
```

time: 71.1 us -> 64.4 us (0.906); the launches traced: 70 us -> 64.4 us
  Pallas kernels: 66.9 us -> 62 us
    pallas_call x1, Pallas kernels: 66.9 us -> 62 us  [body(): pl.pallas_call(kernel, out_shape=jax.ShapeDtypeStruct(block, f32), in_spe...]
    unnamed x3 -> x1, local copies, waits for them, and re-layouts: 2.36 us -> 1.71 us
where the time goes in v2:
time: 64.4 us
  Pallas kernels  62 us (96%)
  local copies, waits for them, and re-layouts  1.71 us (3%)
  between operations  0.66 us (1%)
    pallas_call x1, Pallas kernels, body(): pl.pallas_call(kernel, out_shape=jax.ShapeDtypeStruct(block, f32), in_spe...  62 us
    unnamed x1, local copies, waits for them, and re-layouts  1.71 us

profile of v2, /device:TPU:224, one launch (start us, length us, event | category | flops | bytes accessed | tf_op | source)
XLA Modules:
  0.0 64.4 jit_solution(5369705303213680734)
XLA Ops:
  0.7 62.0 %substep.1 = f32[25,8,32,128]{3,2,1,0:T(8,128)S(1)} custom-call(f32[25,8,32,128]{3,2,1,0:T(8,128)} %sec.1, f32[25,8,32,128]{3,2,1,0:T(8,128)} %base.1, s32[1,1]{1,0:T(1,128)S(6)} %copy.5.flag), custom_call_target="tpu_custom_call" | custom-call | flops 80000000 | bytes 9830400 | tf_op jit(solution)/shard_map/substep/pallas_call | solution.py:470
  62.6 1.7 %copy.6 = f32[25,8,32,128]{3,2,1,0:T(8,128)} copy(f32[25,8,32,128]{3,2,1,0:T(8,128)S(1)} %substep.1) | data formatting | bytes 6553600

commit v3 on v2

--- a/solution.py
+++ b/solution.py
@@ -12,6 +12,7 @@
 NEGATIVE_BITS = sum(1 << c for c in NEGATIVE)
 FIRST = (17, 19, 20, 21)
 EARLY = 8
+NEAR = 2
 ROWS_Z, ROWS_X, ROWS_Y = 8, 32, 128
 TILES = ROWS_X // 8
 STEP = 0.25
@@ -76,9 +77,9 @@
 
 
 def kernel(
-    sec, base, flag, out,
-    pad, acc, cross, packed, from_left, from_right, flag_at,
-    load_sem, store_sem, z_send, z_recv, x_send, x_recv, y_send, y_recv, leg_send, leg_recv, arrive_recv, hello,
+    sec, base, flag, acc,
+    pad, cross, packed, from_left, from_right, flag_at,
+    load_sem, z_send, z_recv, x_send, x_recv, y_send, y_recv, leg_send, leg_recv, arrive_recv, hello,
 ):
     gx, gy, gz = lax.axis_index("gx"), lax.axis_index("gy"), lax.axis_index("gz")
     low, z, core = gx // 8, gx % 8, gy % 2
@@ -93,17 +94,16 @@
     load_s = pltpu.make_async_copy(sec, pad.at[:, 3:11, 8:40, :], load_sem.at[0])
     load_b = pltpu.make_async_copy(base, acc, load_sem.at[1])
     load_f = pltpu.make_async_copy(flag, flag_at, load_sem.at[2])
+    barrier = pltpu.get_barrier_semaphore()
+
+    def tell(semaphore, device):
+        pl.semaphore_signal(semaphore, inc=1, device_id=device, device_id_type=MESH)
+
+    tell(barrier, partner)
     load_s.start()
     load_b.start()
     load_f.start()
 
-    barrier = pltpu.get_barrier_semaphore()
-
-    def tell(semaphore, device):
-        pl.semaphore_signal(semaphore, inc=1, device_id=device, device_id_type=MESH)
-
-    tell(barrier, partner)
-
     @pl.when(core == 1)
     def _():
         tell(barrier, left)
@@ -117,20 +117,24 @@
     def _():
         tell(barrier, up)
 
-    @pl.when(gx != 7)
+    @pl.when(z < NEAR)
     def _():
         tell(barrier, last)
 
+    @pl.when(gx == 0)
+    def _():
+        tell(barrier, first)
+
     @pl.when(is_first)
     def _():
         for q in range(8):
-            tell(barrier, in_row(0, q))
             if q > 0:
+                tell(barrier, in_row(0, q))
                 tell(barrier, in_row(1, q))
 
     expected = (
         1 + jnp.where(core == 0, 2, 0) + jnp.where((core == 0) & (gx == 0), 1, 0) + jnp.where(z > 0, 1, 0)
-        + jnp.where(is_last, 15, 0) + jnp.where(is_first, 0, 1)
+        + jnp.where(is_last, 2 * NEAR, 0) + jnp.where(gx == 0, 0, 1)
     )
     pl.semaphore_wait(barrier, expected)
 
@@ -159,14 +163,15 @@
     def _():
         tell(hello.at[2], mirror)
 
-    @pl.when(low == 0)
+    @pl.when(((low == 0) & (z > 0)) | (z >= NEAR))
     def _():
         tell(hello.at[3], first)
 
     @pl.when(is_last)
     def _():
-        for q in range(7):
+        for q in range(NEAR):
             tell(hello.at[4], in_row(0, q))
+        tell(hello.at[5], first)
 
     to_up = remote(sec.at[:, :, 29:32, :], pad.at[:, 3:11, 5:8, :], x_send.at[3], x_recv.at[3], up)
     to_down = remote(sec.at[:, :, 0:3, :], pad.at[:, 3:11, 40:43, :], x_send.at[4], x_recv.at[4], down)
@@ -200,7 +205,7 @@
 
     @pl.when(is_last)
     def _():
-        for q in range(8):
+        for q in range(NEAR):
             leg_out(0, q).start()
 
     lane = lax.broadcasted_iota(jnp.int32, (8, 128), 1)
@@ -237,6 +242,16 @@
         pl.semaphore_wait(hello.at[0], 1)
         to_up.start()
 
+    def start_rest():
+        @pl.loop(EARLY, FIELDS)
+        def _(n):
+            for copy in z_copies(n):
+                copy.start()
+
+    @pl.when((gx != 7) & (gx != 8))
+    def _():
+        start_rest()
+
     @pl.when((core == 1) & (gx == 0))
     def _():
         pl.semaphore_wait(hello.at[2], 1)
@@ -248,18 +263,36 @@
 
     @pl.when(is_first)
     def _():
-        pl.semaphore_wait(hello.at[3], 8)
+        pl.semaphore_wait(hello.at[3], 15 - NEAR)
         for q in range(8):
             leg_out(1, q).start()
-
-    @pl.loop(EARLY, FIELDS)
-    def _(n):
-        for copy in z_copies(n):
-            copy.start()
+        pl.semaphore_wait(hello.at[5], 1)
+        for q in range(NEAR, 8):
+            tell(hello.at[4], in_row(1, q))
+        start_rest()
+
+    @pl.when((low == 1) & (z >= NEAR))
+    def _():
+        pl.semaphore_wait(hello.at[4], 1)
+        tell(hello.at[5], last)
+
+    @pl.when(is_last)
+    def _():
+        pl.semaphore_wait(hello.at[5], 8 - NEAR)
+        for q in range(NEAR, 8):
+            leg_out(0, q).start()
+        start_rest()
+
+    @pl.when(gx < 6)
+    def _():
+        pl.semaphore_wait(hello.at[4], 1)
+
+    @pl.when((gx > NEAR) & (gx < 7))
+    def _():
+        tell(hello.at[4], down)
 
     @pl.when(gx < 7)
     def _():
-        pl.semaphore_wait(hello.at[4], 1)
         leg_out(1, 0).wait_recv()
         leg_in(1).start()
 
@@ -404,9 +437,6 @@
                 at = (f, z, pl.ds(row, 8), slice(None))
                 acc[at] = acc[at] + (bz * dz + damp * smooth)
 
-    def store(f):
-        return pltpu.make_async_copy(acc.at[f], out.at[f], store_sem.at[f])
-
     @pl.loop(0, FIELDS)
     def _(n):
         @pl.when(n >= len(FIRST))
@@ -414,12 +444,7 @@
             for copy in z_copies(n):
                 copy.wait_recv()
 
-        f = field_at(n)
-        along_z(f)
-        store(f).start()
-
-    @pl.loop(0, FIELDS)
-    def _(n):
+        along_z(field_at(n))
         for copy in z_copies(n):
             copy.wait_send()
 
@@ -457,10 +482,6 @@
     @pl.when(gy < 7)
     def _():
         to_right.wait_send()
-
-    @pl.loop(0, FIELDS)
-    def _(f):
-        store(f).wait()
 
 
 def body(section_fields, base_fields, flags):
@@ -475,17 +496,15 @@
             pl.BlockSpec(memory_space=pl.ANY),
             pl.BlockSpec(memory_space=pl.ANY),
         ],
-        out_specs=pl.BlockSpec(memory_space=pl.ANY),
+        out_specs=pl.BlockSpec(memory_space=pltpu.VMEM),
         scratch_shapes=[
             pltpu.VMEM((FIELDS, 14, 48, ROWS_Y), f32),
-            pltpu.VMEM(block, f32),
             pltpu.VMEM((FIELDS, 8, ROWS_Y), f32),
             pltpu.VMEM((2, ROWS_Z, ROWS_X, ROWS_Y), f32),
             pltpu.VMEM((2, ROWS_Z, ROWS_X, ROWS_Y), f32),
             pltpu.VMEM((2, ROWS_Z, ROWS_X, ROWS_Y), f32),
             pltpu.SMEM((1, 1), jnp.int32),
             dma((3,)),
-            dma((FIELDS,)),
             dma((2, FIELDS)),
             dma((2, FIELDS)),
             dma((5,)),
@@ -495,7 +514,7 @@
             dma((9,)),
             dma((1,)),
             dma((8,)),
-            pltpu.SemaphoreType.REGULAR((5,)),
+            pltpu.SemaphoreType.REGULAR((6,)),
         ],
         compiler_params=pltpu.CompilerParams(
             collective_id=0, has_side_effects=True, vmem_limit_bytes=48 * 2**20

time: 64.4 us -> 62.2 us (0.966)
  Pallas kernels: 62 us -> 59.7 us
    pallas_call x1, Pallas kernels: 62 us -> 59.7 us  [body(): pl.pallas_call(kernel, out_shape=jax.ShapeDtypeStruct(block, f32), in_spe...]
where the time goes in v3:
time: 62.2 us; the launch traced here: 62.1 us
  Pallas kernels  59.7 us (96%)
  local copies, waits for them, and re-layouts  1.71 us (3%)
  between operations  0.66 us (1%)
    pallas_call x1, Pallas kernels, body(): pl.pallas_call(kernel, out_shape=jax.ShapeDtypeStruct(block, f32), in_spe...  59.7 us
    unnamed x1, local copies, waits for them, and re-layouts  1.71 us

profile of v3, /device:TPU:224, one launch (start us, length us, event | category | flops | bytes accessed | tf_op | source)
XLA Modules:
  0.0 62.1 jit_solution(17998368240618054415)
XLA Ops:
  0.7 59.7 %substep.1 = f32[25,8,32,128]{3,2,1,0:T(8,128)S(1)} custom-call(f32[25,8,32,128]{3,2,1,0:T(8,128)} %sec.1, f32[25,8,32,128]{3,2,1,0:T(8,128)} %base.1, s32[1,1]{1,0:T(1,128)S(6)} %copy.5.flag), custom_call_target="tpu_custom_call" | custom-call | flops 80000000 | bytes 9830400 | tf_op jit(solution)/shard_map/substep/pallas_call | solution.py:491
  60.4 1.7 %copy.6 = f32[25,8,32,128]{3,2,1,0:T(8,128)} copy(f32[25,8,32,128]{3,2,1,0:T(8,128)S(1)} %substep.1) | data formatting | bytes 6553600

commit v4 on v3

--- a/solution.py
+++ b/solution.py
@@ -100,8 +100,6 @@
         pl.semaphore_signal(semaphore, inc=1, device_id=device, device_id_type=MESH)
 
     tell(barrier, partner)
-    load_s.start()
-    load_b.start()
     load_f.start()
 
     @pl.when(core == 1)
@@ -113,9 +111,14 @@
     def _():
         tell(barrier, mirror)
 
-    @pl.when(z < 7)
+    @pl.when(z < 4)
     def _():
         tell(barrier, up)
+
+    @pl.when(z == 0)
+    def _():
+        for q in range(4, 8):
+            tell(barrier, (gx + q, gy, gz))
 
     @pl.when(z < NEAR)
     def _():
@@ -133,7 +136,7 @@
                 tell(barrier, in_row(1, q))
 
     expected = (
-        1 + jnp.where(core == 0, 2, 0) + jnp.where((core == 0) & (gx == 0), 1, 0) + jnp.where(z > 0, 1, 0)
+        1 + jnp.where(core == 0, 2, 0) + jnp.where((core == 0) & (gx == 0), 1, 0) + jnp.where(z > 0, 1, 0) + jnp.where(z == 4, 1, 0)
         + jnp.where(is_last, 2 * NEAR, 0) + jnp.where(gx == 0, 0, 1)
     )
     pl.semaphore_wait(barrier, expected)
@@ -150,9 +153,25 @@
         for copy in z_copies(n):
             copy.start()
 
-    @pl.when(z > 0)
+    def start_rest():
+        @pl.loop(EARLY, FIELDS)
+        def _(n):
+            for copy in z_copies(n):
+                copy.start()
+
+    @pl.when((gx != 7) & (gx != 8))
+    def _():
+        start_rest()
+
+    load_s.start()
+
+    @pl.when((z > 0) & (z < 5))
     def _():
         tell(hello.at[0], down)
+
+    @pl.when(z > 3)
+    def _():
+        tell(hello.at[0], (gx - z, gy, gz))
 
     @pl.when(core == 0)
     def _():
@@ -199,7 +218,7 @@
     def piece(half, q):
         return remote(cross.at[:, 0:3, :], piece_ghost(half, q), leg_send.at[8], arrive_recv.at[q], first)
 
-    @pl.when(z > 0)
+    @pl.when((z > 0) & (z < 5))
     def _():
         to_down.start()
 
@@ -237,20 +256,23 @@
     def _():
         to_right.start()
 
+    @pl.when(z == 0)
+    def _():
+        pl.semaphore_wait(hello.at[0], 5)
+        for q in range(4, 8):
+            tell(hello.at[0], (gx + q, gy, gz))
+
+    @pl.when(z > 0)
+    def _():
+        pl.semaphore_wait(hello.at[0], 1)
+
     @pl.when(z < 7)
     def _():
-        pl.semaphore_wait(hello.at[0], 1)
         to_up.start()
 
-    def start_rest():
-        @pl.loop(EARLY, FIELDS)
-        def _(n):
-            for copy in z_copies(n):
-                copy.start()
-
-    @pl.when((gx != 7) & (gx != 8))
-    def _():
-        start_rest()
+    @pl.when(z > 4)
+    def _():
+        to_down.start()
 
     @pl.when((core == 1) & (gx == 0))
     def _():
@@ -300,6 +322,8 @@
     def _():
         leg_out(0, 1).wait_recv()
         leg_in(0).start()
+
+    load_b.start()
 
     place = lax.broadcasted_iota(jnp.int32, (ROWS_X, 128), 1) % 8
 
@@ -424,6 +448,41 @@
     def _(i):
         tile(i // 2, pl.multiple_of(24 * (i % 2), 8))
 
+    @pl.when(z > 0)
+    def _():
+        to_down.wait_send()
+
+    @pl.when(z < 7)
+    def _():
+        to_up.wait_send()
+
+    @pl.when(gx == 0)
+    def _():
+        for copy in to_mirror:
+            copy.wait_send()
+
+    @pl.when(is_last)
+    def _():
+        for q in range(8):
+            leg_out(0, q).wait_send()
+
+    @pl.when(is_first)
+    def _():
+        for q in range(8):
+            leg_out(1, q).wait_send()
+
+    @pl.when((gx != 7) & (gx != 8))
+    def _():
+        piece(0, 0).wait_send()
+
+    @pl.when(gy > 0)
+    def _():
+        to_left.wait_send()
+
+    @pl.when(gy < 7)
+    def _():
+        to_right.wait_send()
+
     def along_z(f):
         @pl.loop(0, TILES)
         def _(t):
@@ -447,41 +506,6 @@
         along_z(field_at(n))
         for copy in z_copies(n):
             copy.wait_send()
-
-    @pl.when(z > 0)
-    def _():
-        to_down.wait_send()
-
-    @pl.when(z < 7)
-    def _():
-        to_up.wait_send()
-
-    @pl.when(gx == 0)
-    def _():
-        for copy in to_mirror:
-            copy.wait_send()
-
-    @pl.when(is_last)
-    def _():
-        for q in range(8):
-            leg_out(0, q).wait_send()
-
-    @pl.when(is_first)
-    def _():
-        for q in range(8):
-            leg_out(1, q).wait_send()
-
-    @pl.when((gx != 7) & (gx != 8))
-    def _():
-        piece(0, 0).wait_send()
-
-    @pl.when(gy > 0)
-    def _():
-        to_left.wait_send()
-
-    @pl.when(gy < 7)
-    def _():
-        to_right.wait_send()
 
 
 def body(section_fields, base_fields, flags):

time: 62.2 us -> 62 us (level)
  no operation moved by 1% of the time
where the time goes in v4:
time: 62 us; the launch traced here: 61.5 us
  Pallas kernels  59.2 us (95%)
  local copies, waits for them, and re-layouts  1.71 us (3%)
  between operations  0.66 us (1%)
    pallas_call x1, Pallas kernels, body(): pl.pallas_call(kernel, out_shape=jax.ShapeDtypeStruct(block, f32), in_spe...  59.2 us
    unnamed x1, local copies, waits for them, and re-layouts  1.71 us

profile of v4, /device:TPU:224, one launch (start us, length us, event | category | flops | bytes accessed | tf_op | source)
XLA Modules:
  0.0 61.5 jit_solution(6421617377673550059)
XLA Ops:
  0.7 59.2 %substep.1 = f32[25,8,32,128]{3,2,1,0:T(8,128)S(1)} custom-call(f32[25,8,32,128]{3,2,1,0:T(8,128)} %sec.1, f32[25,8,32,128]{3,2,1,0:T(8,128)} %base.1, s32[1,1]{1,0:T(1,128)S(6)} %copy.5.flag), custom_call_target="tpu_custom_call" | custom-call | flops 80000000 | bytes 9830400 | tf_op jit(solution)/shard_map/substep/pallas_call | solution.py:515
  59.8 1.7 %copy.6 = f32[25,8,32,128]{3,2,1,0:T(8,128)} copy(f32[25,8,32,128]{3,2,1,0:T(8,128)S(1)} %substep.1) | data formatting | bytes 6553600

commit v5 on v4

--- a/solution.py
+++ b/solution.py
@@ -484,9 +484,7 @@
         to_right.wait_send()
 
     def along_z(f):
-        @pl.loop(0, TILES)
-        def _(t):
-            row = pl.multiple_of(t * 8, 8)
+        for row in range(0, ROWS_X, 8):
             v = [pad[f, z, pl.ds(row + 8, 8), :] for z in range(14)]
             for z in range(8):
                 w = v[z:z + 7]

time: 62 us -> 62 us (level)
  no operation moved by 1% of the time
where the time goes in v5:
time: 62 us; the launch traced here: 61.5 us
  Pallas kernels  59.1 us (95%)
  local copies, waits for them, and re-layouts  1.71 us (3%)
  between operations  0.66 us (1%)
    pallas_call x1, Pallas kernels, body(): pl.pallas_call(kernel, out_shape=jax.ShapeDtypeStruct(block, f32), in_spe...  59.1 us
    unnamed x1, local copies, waits for them, and re-layouts  1.71 us

profile of v5, /device:TPU:224, one launch (start us, length us, event | category | flops | bytes accessed | tf_op | source)
XLA Modules:
  0.0 61.5 jit_solution(12477350207415533085)
XLA Ops:
  0.7 59.1 %substep.1 = f32[25,8,32,128]{3,2,1,0:T(8,128)S(1)} custom-call(f32[25,8,32,128]{3,2,1,0:T(8,128)} %sec.1, f32[25,8,32,128]{3,2,1,0:T(8,128)} %base.1, s32[1,1]{1,0:T(1,128)S(6)} %copy.5.flag), custom_call_target="tpu_custom_call" | custom-call | flops 80000000 | bytes 9830400 | tf_op jit(solution)/shard_map/substep/pallas_call | solution.py:513
  59.8 1.7 %copy.6 = f32[25,8,32,128]{3,2,1,0:T(8,128)} copy(f32[25,8,32,128]{3,2,1,0:T(8,128)S(1)} %substep.1) | data formatting | bytes 6553600

commit v6 on v5

--- a/solution.py
+++ b/solution.py
@@ -483,9 +483,12 @@
     def _():
         to_right.wait_send()
 
-    def along_z(f):
+    @pl.loop(0, FIELDS)
+    def _(f):
         for row in range(0, ROWS_X, 8):
-            v = [pad[f, z, pl.ds(row + 8, 8), :] for z in range(14)]
+            own = [pad[f, z, pl.ds(row + 8, 8), :] for z in range(3, 11)]
+            none = [jnp.zeros((8, 128), jnp.float32)] * 3
+            v = none + own + none
             for z in range(8):
                 w = v[z:z + 7]
                 bz = pad[21, z + 3, pl.ds(row + 8, 8), :] * (STEP / 12.0)
@@ -493,6 +496,20 @@
                 smooth = (w[6] + w[0]) - 6.0 * (w[5] + w[1]) + 15.0 * (w[4] + w[2]) - 20.0 * w[3]
                 at = (f, z, pl.ds(row, 8), slice(None))
                 acc[at] = acc[at] + (bz * dz + damp * smooth)
+
+    def along_z(f):
+        for row in range(0, ROWS_X, 8):
+            for side, edge in ((-1, 0), (1, 7)):
+                g = [pad[f, edge + 3 + side * k, pl.ds(row + 8, 8), :] for k in (1, 2, 3)]
+                b = [pad[21, edge + 3 - side * k, pl.ds(row + 8, 8), :] * (side * STEP / 12.0) for k in (0, 1)]
+                parts = (
+                    b[0] * (8.0 * g[0] - g[1]) + damp * (g[2] - 6.0 * g[1] + 15.0 * g[0]),
+                    damp * (g[1] - 6.0 * g[0]) - b[1] * g[0],
+                    damp * g[0],
+                )
+                for k, part in enumerate(parts):
+                    at = (f, edge - side * k, pl.ds(row, 8), slice(None))
+                    acc[at] = acc[at] + part
 
     @pl.loop(0, FIELDS)
     def _(n):

time: 62 us -> 61.9 us (level)
  no operation moved by 1% of the time
where the time goes in v6:
time: 61.9 us; the launch traced here: 61.5 us
  Pallas kernels  59.1 us (95%)
  local copies, waits for them, and re-layouts  1.71 us (3%)
  between operations  0.66 us (1%)
    pallas_call x1, Pallas kernels, body(): pl.pallas_call(kernel, out_shape=jax.ShapeDtypeStruct(block, f32), in_spe...  59.1 us
    unnamed x1, local copies, waits for them, and re-layouts  1.71 us

profile of v6, /device:TPU:224, one launch (start us, length us, event | category | flops | bytes accessed | tf_op | source)
XLA Modules:
  0.0 61.5 jit_solution(17080993047150346565)
XLA Ops:
  0.7 59.1 %substep.1 = f32[25,8,32,128]{3,2,1,0:T(8,128)S(1)} custom-call(f32[25,8,32,128]{3,2,1,0:T(8,128)} %sec.1, f32[25,8,32,128]{3,2,1,0:T(8,128)} %base.1, s32[1,1]{1,0:T(1,128)S(6)} %copy.5.flag), custom_call_target="tpu_custom_call" | custom-call | flops 80000000 | bytes 9830400 | tf_op jit(solution)/shard_map/substep/pallas_call | solution.py:530
  59.8 1.7 %copy.6 = f32[25,8,32,128]{3,2,1,0:T(8,128)} copy(f32[25,8,32,128]{3,2,1,0:T(8,128)S(1)} %substep.1) | data formatting | bytes 6553600
